TPU v7x, 256 devices: a whole 4x4x8 slice. The times are simulated.
256 devices in a mesh: grid: 32 (over z, y), var: 8 (over x, core).
Axes of the slice: x: 4, y: 4, z: 8, core: 2. Of those that a mesh axis runs over, the one named last changes fastest.
Arguments:
- tensor_field: float32 [16, 512, 32768], P('var', None, 'grid'), may hold values from -400 to 400, as said below
- start_basis: float32 [512, 128], replicated, may hold values from -6 to 6
Outputs:
- core_tensor: float32 [16, 128, 32768], P('var', None, 'grid')
- factor_basis: float32 [512, 128], replicated
Inputs may be any that keep to these rules, and one draw needn't show every extreme that they name: `tensor_field`: Real-valued field of variables with differing scales.
All inputs are finite; a program needn't handle non-finite values.
Results may differ from a plain program's by a relative error of at most 0.0003.
Values sent between devices are 32-bit elements; how exact they have to be, the bound alone decides.
No kernel may reach another device: no remote copies, remote signals or barrier semaphores. Data moves between devices by JAX's collectives and lax.ppermute only.
A program may use at most 64 MiB of HBM per device.

v0:
```python
import jax
import jax.numpy as jnp
from jax import lax
from jax.sharding import PartitionSpec as P

ITERS = 4


def orthonormal(image_rows, products):
    factor = jnp.linalg.cholesky(products)
    return jax.scipy.linalg.solve_triangular(factor, image_rows.T, lower=True).T


def local(tensor_field, start_basis):
    highest = lax.Precision.HIGHEST
    column_total = (
        tensor_field.shape[0] * tensor_field.shape[2] * lax.axis_size("grid") * lax.axis_size("var")
    )
    current_basis = start_basis
    partial_gram = (
        lax.dot_general(tensor_field, tensor_field, (((0, 2), (0, 2)), ((), ())), precision=highest)
        / column_total
    )
    gram_full = lax.psum(partial_gram, ("grid", "var"))
    for iteration in range(ITERS):
        image_rows = jnp.dot(gram_full, current_basis, precision=highest)
        products = jnp.dot(image_rows.T, image_rows, precision=highest)
        current_basis = orthonormal(image_rows, products)
    core_tensor = jnp.einsum("ir,vic->vrc", current_basis, tensor_field, precision=highest)
    return (core_tensor, current_basis)


def solution(mesh):
    return jax.shard_map(
        local,
        mesh=mesh,
        in_specs=(P("var", None, "grid"), P()),
        out_specs=(P("var", None, "grid"), P()),
        check_vma=False,
    )
```

profile of v0, /device:TPU:1, one launch (start us, length us, event | category | flops | bytes accessed | tf_op | source)
XLA Modules:
  0.0 392.9 jit_solution(11389150873923204176)
XLA Ops:
  7.2 0.0 copy-start
  7.2 0.0 all-reduce.2.cloned.1.call-start
  7.2 10.6 %fusion = f32[512,512]{1,0:T(8,128)} fusion(f32[2,512,1024]{2,1,0:T(8,128)} %param.5), kind=kOutput, calls=%fused_computation.2 | convolution fusion | flops 6442713088 | bytes 5242880 | tf_op jit(solution)/shard_map/dot_general | solution.py:21
  17.9 0.0 all-reduce.2.cloned.1.call-update
  17.9 258.4 %all-reduce.2.cloned.1.call-done = f32[512,512]{1,0:T(8,128)} async-done(((f32[512,512]{1,0:T(8,128)}), f32[512,512]{1,0:T(8,128)}) %all-reduce.2.cloned.1.call-update) | async-done | bytes 1048592 | tf_op jit(solution)/shard_map/psum | solution.py:24
  276.3 0.0 copy-done
  276.3 0.0 copy-start.1
  276.4 2.3 fusion.28
  278.7 0.6 fusion.29
  279.2 0.1 copy.4
  279.4 11.7 %cholesky.74 = f32[128,128]{1,0:T(8,128)S(1)} custom-call(f32[128,128]{1,0:T(8,128)S(1)} %fusion.21), custom_call_target="Cholesky" | custom-call | tf_op jit(solution)/shard_map/jit(cholesky)/cholesky | solution.py:10
  291.1 0.6 compare_reduce_fusion.3
  291.8 0.7 fusion.10
  292.4 9.8 %custom-call.8 = f32[1,128,128]{1,2,0:T(8,128)S(1)} custom-call(f32[1,128,128]{2,1,0:T(8,128)S(1)} %fusion.10), custom_call_target="InvertDiagBlocksLowerTriangular" | custom-call | tf_op jit(solution)/shard_map/jit(_solve_triangular)/triangular_solve | solution.py:11
  302.2 0.4 fusion.8
  302.7 2.2 fusion.30
  304.9 0.6 fusion.31
  305.5 0.1 copy.5
  305.6 11.9 %cholesky.85 = f32[128,128]{1,0:T(8,128)S(1)} custom-call(f32[128,128]{1,0:T(8,128)S(1)} %fusion.19), custom_call_target="Cholesky" | custom-call | tf_op jit(solution)/shard_map/jit(cholesky)/cholesky | solution.py:10
  317.5 0.6 compare_reduce_fusion.2
  318.2 0.7 fusion.11
  318.8 9.8 %custom-call.9 = f32[1,128,128]{1,2,0:T(8,128)S(1)} custom-call(f32[1,128,128]{2,1,0:T(8,128)S(1)} %fusion.11), custom_call_target="InvertDiagBlocksLowerTriangular" | custom-call | tf_op jit(solution)/shard_map/jit(_solve_triangular)/triangular_solve | solution.py:11
  328.7 0.4 fusion.6
  329.1 0.0 copy-done.1
  329.1 1.0 fusion.32
  330.1 0.6 fusion.33
  330.7 0.1 copy.6
  330.8 11.7 %cholesky.96 = f32[128,128]{1,0:T(8,128)S(1)} custom-call(f32[128,128]{1,0:T(8,128)S(1)} %fusion.17), custom_call_target="Cholesky" | custom-call | tf_op jit(solution)/shard_map/jit(cholesky)/cholesky | solution.py:10
  342.5 0.6 compare_reduce_fusion.1
  343.2 0.7 fusion.12
  343.8 9.8 %custom-call.10 = f32[1,128,128]{1,2,0:T(8,128)S(1)} custom-call(f32[1,128,128]{2,1,0:T(8,128)S(1)} %fusion.12), custom_call_target="InvertDiagBlocksLowerTriangular" | custom-call | tf_op jit(solution)/shard_map/jit(_solve_triangular)/triangular_solve | solution.py:11
  353.7 0.4 fusion.4
  354.1 1.2 fusion.34
  355.3 0.6 fusion.35
  355.9 0.1 copy.7
  356.0 11.7 %cholesky.107 = f32[128,128]{1,0:T(8,128)S(1)} custom-call(f32[128,128]{1,0:T(8,128)S(1)} %fusion.15), custom_call_target="Cholesky" | custom-call | tf_op jit(solution)/shard_map/jit(cholesky)/cholesky | solution.py:10
  367.8 0.6 compare_reduce_fusion
  368.4 0.7 fusion.13
  369.1 9.8 %custom-call.11 = f32[1,128,128]{1,2,0:T(8,128)S(1)} custom-call(f32[1,128,128]{2,1,0:T(8,128)S(1)} %fusion.13), custom_call_target="InvertDiagBlocksLowerTriangular" | custom-call | tf_op jit(solution)/shard_map/jit(_solve_triangular)/triangular_solve | solution.py:11
  378.9 0.4 fusion.2
  379.3 5.5 %convolution_bitcast_fusion = f32[2,128,1024]{2,1,0:T(8,128)} fusion(f32[2,512,1024]{2,1,0:T(8,128)} %param.5, f32[128,512]{1,0:T(8,128)S(1)} %fusion.2), kind=kOutput, calls=%fused_computation | convolution fusion | flops 1610612736 | bytes 5505024 | tf_op jit(solution)/shard_map/ir,vic->vrc/dot_general | solution.py:29
  384.8 0.8 copy.8
  (8 shorter events, 0.2 us)
Async XLA Ops:
  7.2 269.2 %copy-start = (f32[512,128]{1,0:T(8,128)S(1)}, f32[512,128]{1,0:T(8,128)}, u32[]{:S(2)}) copy-start(f32[512,128]{1,0:T(8,128)} %param.6) | copy-start | bytes 786436
  7.2 269.2 %all-reduce.2.cloned.1.call-start = ((), (), s32[]{:S(2)}) async-start(), calls=%async_computation | async-start | bytes 2097152 | tf_op jit(solution)/shard_map/psum | solution.py:24
  276.3 52.7 %copy-start.1 = (f32[512,512]{1,0:T(8,128)S(1)}, f32[512,512]{1,0:T(8,128)}, u32[]{:S(2)}) copy-start(f32[512,512]{1,0:T(8,128)} %all-reduce.2.cloned.1.call-done) | copy-start | bytes 3145732
Sparse Core Ops, SparseCore 0:
  18.0 258.2 all-reduce.1
where the time goes:
time: 397 us; the launch traced here: 393 us
  waiting for transfers between devices  258 us (65%)
  other arithmetic  91.7 us (23%)
  matrix products  26.9 us (7%)
  between operations  14.7 us (4%)
    psum x1, waiting for transfers between devices, local(): gram_full = lax.psum(partial_gram, ('grid', 'var'))  258 us
    another operation x12, other arithmetic, orthonormal(): factor = jnp.linalg.cholesky(products)  49.7 us
    another operation x8, other arithmetic, orthonormal(): return jax.scipy.linalg.solve_triangular(factor, image_rows.T, lower=True).T  41.9 us
    dot_general x1, matrix products, local(): lax.dot_general(tensor_field, tensor_field, (((0, 2), (0, 2)), ((), ())),...  10.6 us
  transfers between devices with their start and end apart: 1, of which 1 were waited for; matrix products, arithmetic and copies ran while one was open for 0% of the time, Pallas kernels for 0%

commit v1 on v0

v1 whole, which is shorter than its diff:
```python
import jax
import jax.numpy as jnp
from jax import lax
from jax.experimental import pallas as pl
from jax.experimental.pallas import tpu as pltpu
from jax.sharding import Mesh, PartitionSpec as P

ITERS = 4
N1 = 512
RANK = 128
PANEL = 16
BLOCK = 128
PAIRS = [(i, j) for i in range(N1 // BLOCK) for j in range(i, N1 // BLOCK)]
HIGHEST = lax.Precision.HIGHEST
STEP = 512


def split(values):
    high = values.astype(jnp.bfloat16)
    low = (values - high.astype(jnp.float32)).astype(jnp.bfloat16)
    return high, low


def dot(left, right, contract):
    return lax.dot_general(left, right, (contract, ((), ())), preferred_element_type=jnp.float32)


def gram_kernel(field_ref, out_ref, total_ref):
    step = pl.program_id(0)
    high, low = split(field_ref[0])
    half = N1 // 2
    nt = ((1,), (1,))

    @pl.when(step == 0)
    def _():
        total_ref[...] = jnp.zeros_like(total_ref)

    total_ref[0] += dot(high[:half], high[:half], nt)
    total_ref[1] += dot(high[half:], high[half:], nt)
    total_ref[2] += dot(high[:half], low[:half], nt)
    total_ref[3] += dot(high[half:], low[half:], nt)
    total_ref[4] += (
        dot(high[:half], high[half:], nt) + dot(high[:half], low[half:], nt) + dot(low[:half], high[half:], nt)
    )

    @pl.when(step == pl.num_programs(0) - 1)
    def _():
        scale = 1.0 / 524288
        top = total_ref[0] + total_ref[2] + total_ref[2].T
        low_corner = total_ref[1] + total_ref[3] + total_ref[3].T
        for index, (i, j) in enumerate(PAIRS):
            if j < 2:
                source = top
            elif i >= 2:
                source = low_corner
            else:
                source = total_ref[4]
            rows = (i % 2) * BLOCK
            columns = (j % 2) * BLOCK
            out_ref[index] = source[rows : rows + BLOCK, columns : columns + BLOCK] * scale


def partial_gram(field):
    variables, _, columns = field.shape
    parts = columns // STEP
    return pl.pallas_call(
        gram_kernel,
        grid=(variables * parts,),
        in_specs=[pl.BlockSpec((1, N1, STEP), lambda s: (s // parts, 0, s % parts))],
        out_specs=pl.BlockSpec((len(PAIRS), BLOCK, BLOCK), lambda s: (0, 0, 0)),
        out_shape=jax.ShapeDtypeStruct((len(PAIRS), BLOCK, BLOCK), jnp.float32),
        scratch_shapes=[pltpu.VMEM((5, N1 // 2, N1 // 2), jnp.float32)],
        compiler_params=pltpu.CompilerParams(vmem_limit_bytes=24 << 20),
    )(field)


def inverse_factor(products):
    panels = RANK // PANEL
    shape = (PANEL, RANK)
    row = lax.broadcasted_iota(jnp.int32, shape, 0)
    lane = lax.broadcasted_iota(jnp.int32, shape, 1)
    rows = [products[PANEL * r : PANEL * (r + 1), :] for r in range(panels)]
    done = []
    for r in range(panels):
        first = PANEL * r
        panel = rows[r]
        columns = [jnp.broadcast_to(panel[:, first + k : first + k + 1], shape) for k in range(PANEL)]
        inside = (lane >= first) & (lane < first + PANEL)
        panel = jnp.where(inside, jnp.where(lane - first == row, 1.0, 0.0), panel)
        scale = jnp.zeros(shape, jnp.float32)
        for k in range(PANEL):
            pivot = jnp.broadcast_to(columns[k][k : k + 1, :], shape)
            scale = jnp.where(row == k, lax.rsqrt(pivot), scale)
            if k < PANEL - 1:
                factor = jnp.where(row > k, columns[k] * (1.0 / pivot), 0.0)
                for j in range(k + 1, PANEL):
                    columns[j] = columns[j] - factor * jnp.broadcast_to(columns[j][k : k + 1, :], shape)
                panel = panel - factor * jnp.broadcast_to(panel[k : k + 1, :], shape)
        panel = panel * scale
        done.append(jnp.where(lane < first + PANEL, panel, 0.0))
        if r == panels - 1:
            break
        after = [jnp.where(inside, 0.0, rows[q]) if q > r else None for q in range(panels)]
        update = jnp.zeros(shape, jnp.float32)
        for i in range(PANEL):
            at = first + PANEL + i
            weights = jnp.broadcast_to(panel[:, at : at + 1], shape)
            total = jnp.sum(weights * panel, axis=0, keepdims=True)
            update = jnp.where(row == i, jnp.broadcast_to(total, shape), update)
        after[r + 1] = after[r + 1] - update
        if r + 2 < panels:
            start = PANEL * (r + 2)
            trail = lax.dot_general(
                panel[:, start:],
                panel,
                (((0,), (0,)), ((), ())),
                precision=HIGHEST,
                preferred_element_type=jnp.float32,
            )
            for q in range(r + 2, panels):
                offset = PANEL * (q - r - 2)
                after[q] = after[q] - trail[offset : offset + PANEL, :]
        rows = after
    return jnp.concatenate(done, axis=0)


def exact_dot(left, right, contract):
    return lax.dot_general(
        left, right, (contract, ((), ())), precision=HIGHEST, preferred_element_type=jnp.float32
    )


def sweeps_kernel(core_ref, own_ref, other_ref, basis_ref, out_ref, gram_ref, image_ref, ahead_ref):
    own_first = core_ref[0] == 0
    rows_half = own_ref.shape[0]
    for index, (i, j) in enumerate(PAIRS):
        at = (index * BLOCK) % rows_half
        own = own_ref[at : at + BLOCK, :]
        other = other_ref[at : at + BLOCK, :]
        in_first = index * BLOCK < rows_half
        block = jnp.where(own_first == in_first, own, other)
        gram_ref[BLOCK * i : BLOCK * (i + 1), BLOCK * j : BLOCK * (j + 1)] = block
        if i != j:
            gram_ref[BLOCK * j : BLOCK * (j + 1), BLOCK * i : BLOCK * (i + 1)] = block.T
    nn = ((1,), (0,))
    image_ref[...] = exact_dot(gram_ref[...], basis_ref[...], nn)

    def sweep(iteration, carry):
        image = image_ref[...]
        products = exact_dot(image, image, ((0,), (0,)))
        ahead_ref[...] = exact_dot(gram_ref[...], image, nn)
        inverse = inverse_factor(products)
        image_ref[...] = exact_dot(ahead_ref[...], inverse, ((1,), (1,)))
        return carry

    lax.fori_loop(0, ITERS - 1, sweep, 0)
    image = image_ref[...]
    products = exact_dot(image, image, ((0,), (0,)))
    inverse = inverse_factor(products)
    out_ref[...] = exact_dot(image, inverse, ((1,), (1,)))


def sweeps(core, own, other, start_basis):
    whole = pl.BlockSpec(memory_space=pltpu.VMEM)
    return pl.pallas_call(
        sweeps_kernel,
        in_specs=[pl.BlockSpec(memory_space=pltpu.SMEM), whole, whole, whole],
        out_specs=whole,
        out_shape=jax.ShapeDtypeStruct((N1, RANK), jnp.float32),
        scratch_shapes=[
            pltpu.VMEM((N1, N1), jnp.float32),
            pltpu.VMEM((N1, RANK), jnp.float32),
            pltpu.VMEM((N1, RANK), jnp.float32),
        ],
        compiler_params=pltpu.CompilerParams(vmem_limit_bytes=24 << 20),
    )(core, own, other, start_basis)


def core_kernel(basis_ref, field_ref, out_ref):
    tn = ((0,), (0,))
    basis_high, basis_low = split(basis_ref[...])
    high, low = split(field_ref[0])
    out_ref[0] = dot(basis_high, high, tn) + dot(basis_high, low, tn) + dot(basis_low, high, tn)


def project(basis, field):
    variables, _, columns = field.shape
    parts = columns // STEP
    return pl.pallas_call(
        core_kernel,
        grid=(variables, parts),
        in_specs=[
            pl.BlockSpec((N1, RANK), lambda v, s: (0, 0)),
            pl.BlockSpec((1, N1, STEP), lambda v, s: (v, 0, s)),
        ],
        out_specs=pl.BlockSpec((1, RANK, STEP), lambda v, s: (v, 0, s)),
        out_shape=jax.ShapeDtypeStruct((variables, RANK, columns), jnp.float32),
        compiler_params=pltpu.CompilerParams(vmem_limit_bytes=24 << 20),
    )(basis, field)


def spread(block, axes, size):
    return lax.all_to_all(jnp.broadcast_to(block, (size,) + block.shape), axes, 0, 0)


def all_sum(packed):
    core = lax.axis_index("core")
    half = packed.shape[0] // 2
    swap = [(0, 1), (1, 0)]
    mine = lax.dynamic_slice_in_dim(packed, core * half, half)
    theirs = lax.dynamic_slice_in_dim(packed, (1 - core) * half, half)
    own = mine + lax.ppermute(theirs, "core", swap)
    plane = lax.axis_size("y") * lax.axis_size("x")
    piece = half // plane
    pieces = lax.all_to_all(own.reshape(plane, piece, BLOCK), ("y", "x"), 0, 0)
    own = jnp.sum(pieces, axis=0)
    own = jnp.sum(spread(own, "z", lax.axis_size("z")), axis=0)
    own = spread(own, ("y", "x"), plane).reshape(half, BLOCK)
    return core, own, lax.ppermute(own, "core", swap)


def local(tensor_field, start_basis):
    packed = partial_gram(tensor_field).reshape(len(PAIRS) * BLOCK, BLOCK)
    core, own, other = all_sum(packed)
    basis = sweeps(core.astype(jnp.int32).reshape(1), own, other, start_basis)
    return project(basis, tensor_field), basis


def solution(mesh):
    fine = Mesh(mesh.devices.reshape(8, 4, 4, 2), ("z", "y", "x", "core"))
    spec = P(("x", "core"), None, ("z", "y"))
    return jax.shard_map(local, mesh=fine, in_specs=(spec, P()), out_specs=(spec, P()), check_vma=False)
```

time: 397 us -> 82.8 us (0.21)
  waiting for transfers between devices: 258 us -> 2.51 us
  other arithmetic: 91.7 us -> 0.07 us
  blocking collectives: 0 us -> 40.9 us
  matrix products: 26.9 us -> 0 us
  Pallas kernels: 0 us -> 25.8 us
  between operations: 14.7 us -> 0.69 us
  starting transfers between devices: 0.04 us -> 7.23 us
  local copies, waits for them, and re-layouts: 1.2 us -> 5.39 us
    psum x1 -> x0, waiting for transfers between devices: 258 us -> none  [local(): gram_full = lax.psum(partial_gram, ('grid', 'var'))]
    another operation x20 -> x0, other arithmetic: 91.6 us -> none  [the longest x12 49.7 us: orthonormal(): factor = jnp.linalg.cholesky(products)]
    all_to_all x0 -> x3, blocking collectives: none -> 40.9 us  [the longest x2 27.2 us: spread(): lax.all_to_all(jnp.broadcast_to(block, (size,) + block.shape), axes, 0, 0)]
    pallas_call x0 -> x3, Pallas kernels: none -> 25.8 us  [the longest x1 18.6 us: sweeps(): pl.pallas_call(sweeps_kernel, in_specs=[pl.BlockSpec(memory_space=pltpu.S...]
    dot_general x10 -> x0, matrix products: 25.2 us -> none  [the longest x1 10.6 us: local(): lax.dot_general(tensor_field, tensor_field, (((0, 2), (0, 2)), ((), ())),...]
    ppermute x0 -> x2, starting transfers between devices: none -> 7.23 us  [the longest x1 3.9 us: all_sum(): return (core, own, lax.ppermute(own, 'core', swap))]
    unnamed x5 -> x8, local copies, waits for them, and re-layouts: 0.85 us -> 5.32 us
  transfers between devices with their start and end apart: 1 -> 2, of which waited for: 1 -> 2; matrix products, arithmetic and copies ran while one was open for 0% -> 0% of each run, Pallas kernels for 0% -> 0%
where the time goes in v1:
time: 82.8 us; the launch traced here: 82.5 us
  blocking collectives  40.9 us (49%)
  Pallas kernels  25.8 us (31%)
  starting transfers between devices  7.23 us (9%)
  local copies, waits for them, and re-layouts  5.39 us (7%)
  waiting for transfers between devices  2.51 us (3%)
    all_to_all x2, blocking collectives, spread(): lax.all_to_all(jnp.broadcast_to(block, (size,) + block.shape), axes, 0, 0)  27.2 us
    pallas_call x1, Pallas kernels, sweeps(): pl.pallas_call(sweeps_kernel, in_specs=[pl.BlockSpec(memory_space=pltpu.S...  18.6 us
    all_to_all x1, blocking collectives, all_sum(): pieces = lax.all_to_all(own.reshape(plane, piece, BLOCK), ('y', 'x'), 0, 0)  13.6 us
    unnamed x8, local copies, waits for them, and re-layouts  5.32 us
    pallas_call x1, Pallas kernels, partial_gram(): pl.pallas_call(gram_kernel, grid=(variables * parts,), in_specs=[pl.Block...  4.2 us
    ppermute x1, starting transfers between devices, all_sum(): return (core, own, lax.ppermute(own, 'core', swap))  3.9 us
    ppermute x1, starting transfers between devices, all_sum(): own = mine + lax.ppermute(theirs, 'core', swap)  3.33 us
    pallas_call x1, Pallas kernels, project(): pl.pallas_call(core_kernel, grid=(variables, parts), in_specs=[pl.BlockSp...  2.98 us
  transfers between devices with their start and end apart: 2, of which 2 were waited for; matrix products, arithmetic and copies ran while one was open for 0% of the time, Pallas kernels for 0%

profile of v1, /device:TPU:1, one launch (start us, length us, event | category | flops | bytes accessed | tf_op | source)
XLA Modules:
  0.0 82.5 jit_solution(12372299586541390853)
XLA Ops:
  0.6 0.0 copy-start
  0.6 2.2 %copy-done = f32[2,512,1024]{2,1,0:T(8,128)S(1)} copy-done((f32[2,512,1024]{2,1,0:T(8,128)S(1)}, f32[2,512,1024]{2,1,0:T(8,128)}, u32[]{:S(2)}) %copy-start) | copy-done | bytes 4194328
  2.8 0.0 copy-start.3
  2.8 4.2 %shard_map.41 = f32[10,128,128]{2,1,0:T(8,128)S(1)} custom-call(f32[2,512,1024]{2,1,0:T(8,128)S(1)} %copy-done), custom_call_target="tpu_custom_call" | custom-call | tf_op jit(solution)/shard_map/pallas_call | solution.py:66
  7.1 3.3 %collective-permute-start = (f32[640,128]{1,0:T(8,128)S(1)}, f32[640,128]{1,0:T(8,128)S(1)}, u32[]{:S(2)}, u32[]{:S(2)}) collective-permute-start(f32[640,128]{1,0:T(8,128)S(1)} %constant_dynamic-slice_fusion), channel_id=1, source_target_pairs={{0,1},{1,0},{2,3},{3,2},{4,5},{5,4},{6,7},{7,6},{8,9},{9,8},{10,11... | collective-permute-start | bytes 983048 | tf_op jit(solution)/shard_map/ppermute | solution.py:212
  10.4 1.3 %collective-permute-done = f32[640,128]{1,0:T(8,128)S(1)} collective-permute-done((f32[640,128]{1,0:T(8,128)S(1)}, f32[640,128]{1,0:T(8,128)S(1)}, u32[]{:S(2)}, u32[]{:S(2)}) %collective-permute-start) | collective-permute-done | bytes 327712 | tf_op jit(solution)/shard_map/ppermute | solution.py:212
  11.7 13.6 %all_to_all.15 = f32[16,40,128]{2,1,0:T(8,128)S(1)} all-to-all(f32[16,40,128]{2,1,0:T(8,128)S(1)} %bitcast.8), channel_id=1, replica_groups=mesh['z'=8,'y'=4,'x'=4,'core'=2] {'y','x'}, dimensions={0} | all-to-all | bytes 655360 | tf_op jit(solution)/shard_map/all_to_all | solution.py:215
  25.4 16.3 %all_to_all.16 = f32[8,40,128]{2,1,0:T(8,128)S(1)} all-to-all(f32[8,40,128]{2,1,0:T(8,128)S(1)} %broadcast_in_dim.6), channel_id=1, replica_groups=mesh['z'=8,'y'=4,'x'=4,'core'=2] {'z'}, dimensions={0} | all-to-all | bytes 327680 | tf_op jit(solution)/shard_map/all_to_all | solution.py:203
  41.7 10.9 %all_to_all.17 = f32[16,40,128]{2,1,0:T(8,128)S(1)} all-to-all(f32[16,40,128]{2,1,0:T(8,128)S(1)} %broadcast_in_dim.7), channel_id=1, replica_groups=mesh['z'=8,'y'=4,'x'=4,'core'=2] {'y','x'}, dimensions={0} | all-to-all | bytes 655360 | tf_op jit(solution)/shard_map/all_to_all | solution.py:203
  52.7 3.9 %collective-permute-start.1 = (f32[640,128]{1,0:T(8,128)S(1)}, f32[640,128]{1,0:T(8,128)S(1)}, u32[]{:S(2)}, u32[]{:S(2)}) collective-permute-start(f32[640,128]{1,0:T(8,128)S(1)} %bitcast.6), channel_id=1, source_target_pairs={{0,1},{1,0},{2,3},{3,2},{4,5},{5,4},{6,7},{7,6},{8,9},{9,8},{10,11... | collective-permute-start | bytes 983048 | tf_op jit(solution)/shard_map/ppermute | solution.py:219
  56.6 1.3 %collective-permute-done.1.other_ref = f32[640,128]{1,0:T(8,128)S(1)} collective-permute-done((f32[640,128]{1,0:T(8,128)S(1)}, f32[640,128]{1,0:T(8,128)S(1)}, u32[]{:S(2)}, u32[]{:S(2)}) %collective-permute-start.1) | collective-permute-done | bytes 327712 | tf_op jit(solution)/shard_map/ppermute | solution.py:219
  57.8 0.0 copy-done.3
  57.8 18.6 %shard_map.42.basis_ref = f32[512,128]{1,0:T(8,128)} custom-call(s32[1]{0:T(128)} %bitcast.core_ref, f32[640,128]{1,0:T(8,128)S(1)} %bitcast.7, f32[640,128]{1,0:T(8,128)S(1)} %collective-permute-done.1.other_ref, f32[512,128]{1,0:T(8,128)S(1)} %copy-done.3), custom_call_target="tpu_custom_call" | custom-call | tf_op jit(solution)/shard_map/pallas_call | solution.py:165
  76.4 0.0 copy-start.1
  76.4 2.2 %copy-done.1 = f32[2,512,1024]{2,1,0:T(8,128)S(1)} copy-done((f32[2,512,1024]{2,1,0:T(8,128)S(1)}, f32[2,512,1024]{2,1,0:T(8,128)}, u32[]{:S(2)}) %copy-start.1) | copy-done | bytes 4194328
  78.6 0.0 copy-start.2
  78.6 0.9 %copy-done.2 = f32[512,128]{1,0:T(8,128)S(1)} copy-done((f32[512,128]{1,0:T(8,128)S(1)}, f32[512,128]{1,0:T(8,128)}, u32[]{:S(2)}) %copy-start.2) | copy-done | bytes 262168
  79.5 3.0 %shard_map.43 = f32[2,128,1024]{2,1,0:T(8,128)} custom-call(f32[512,128]{1,0:T(8,128)S(1)} %copy-done.2, f32[2,512,1024]{2,1,0:T(8,128)S(1)} %copy-done.1), custom_call_target="tpu_custom_call" | custom-call | tf_op jit(solution)/shard_map/pallas_call | solution.py:189
  (6 shorter events, 0.1 us)
Async XLA Ops:
  0.6 2.2 %copy-start = (f32[2,512,1024]{2,1,0:T(8,128)S(1)}, f32[2,512,1024]{2,1,0:T(8,128)}, u32[]{:S(2)}) copy-start(f32[2,512,1024]{2,1,0:T(8,128)} %field_ref.3) | copy-start | bytes 12582916
  2.8 55.0 %copy-start.3 = (f32[512,128]{1,0:T(8,128)S(1)}, f32[512,128]{1,0:T(8,128)}, u32[]{:S(2)}) copy-start(f32[512,128]{1,0:T(8,128)} %basis_ref.1) | copy-start | bytes 786436
  7.1 4.6 %collective-permute-start = (f32[640,128]{1,0:T(8,128)S(1)}, f32[640,128]{1,0:T(8,128)S(1)}, u32[]{:S(2)}, u32[]{:S(2)}) collective-permute-start(f32[640,128]{1,0:T(8,128)S(1)} %constant_dynamic-slice_fusion), channel_id=1, source_target_pairs={{0,1},{1,0},{2,3},{3,2},{4,5},{5,4},{6,7},{7,6},{8,9},{9,8},{10,11... | collective-permute-start | bytes 983048 | tf_op jit(solution)/shard_map/ppermute | solution.py:212
  52.7 5.2 %collective-permute-start.1 = (f32[640,128]{1,0:T(8,128)S(1)}, f32[640,128]{1,0:T(8,128)S(1)}, u32[]{:S(2)}, u32[]{:S(2)}) collective-permute-start(f32[640,128]{1,0:T(8,128)S(1)} %bitcast.6), channel_id=1, source_target_pairs={{0,1},{1,0},{2,3},{3,2},{4,5},{5,4},{6,7},{7,6},{8,9},{9,8},{10,11... | collective-permute-start | bytes 983048 | tf_op jit(solution)/shard_map/ppermute | solution.py:219
  76.4 2.2 %copy-start.1 = (f32[2,512,1024]{2,1,0:T(8,128)S(1)}, f32[2,512,1024]{2,1,0:T(8,128)}, u32[]{:S(2)}) copy-start(f32[2,512,1024]{2,1,0:T(8,128)} %field_ref.3) | copy-start | bytes 12582916
  78.6 0.9 %copy-start.2 = (f32[512,128]{1,0:T(8,128)S(1)}, f32[512,128]{1,0:T(8,128)}, u32[]{:S(2)}) copy-start(f32[512,128]{1,0:T(8,128)} %shard_map.42.basis_ref) | copy-start | bytes 786436

commit v2 on v0

v2 whole, which is shorter than its diff:
```python
import jax
import jax.numpy as jnp
from jax import lax
from jax.experimental import pallas as pl
from jax.experimental.pallas import tpu as pltpu
from jax.sharding import Mesh, PartitionSpec as P

ITERS = 4
N1 = 512
RANK = 128
PANEL = 16
BLOCK = 128
PAIRS = [(i, j) for i in range(N1 // BLOCK) for j in range(i, N1 // BLOCK)]
HIGHEST = lax.Precision.HIGHEST
STEP = 512
TILE = (8, 128)


def split(values):
    high = values.astype(jnp.bfloat16)
    low = (values - high.astype(jnp.float32)).astype(jnp.bfloat16)
    return high, low


def dot(left, right, contract):
    return lax.dot_general(left, right, (contract, ((), ())), preferred_element_type=jnp.float32)


def gram_kernel(field_ref, out_ref, parts_ref, total_ref, arrived):
    nt = ((1,), (1,))
    variables, _, columns = field_ref.shape
    per = columns // STEP
    copies = [
        pltpu.make_async_copy(
            field_ref.at[c // per, :, pl.ds((c % per) * STEP, STEP)], parts_ref.at[c], arrived.at[c]
        )
        for c in range(variables * per)
    ]
    for copy in copies:
        copy.start()
    for c, copy in enumerate(copies):
        copy.wait()
        high, low = split(parts_ref[c])
        halved = high * jnp.bfloat16(0.5)
        term = dot(high, halved, nt) + dot(high, low, nt)
        if c == 0:
            total_ref[...] = term
        else:
            total_ref[...] += term
    scale = 1.0 / 524288
    for index, (i, j) in enumerate(PAIRS):
        rows = pl.ds(BLOCK * i, BLOCK)
        others = pl.ds(BLOCK * j, BLOCK)
        out_ref[index] = (total_ref[rows, others] + total_ref[others, rows].T) * scale


def partial_gram(field):
    variables, _, columns = field.shape
    parts = variables * columns // STEP
    return pl.pallas_call(
        gram_kernel,
        in_specs=[pl.BlockSpec(memory_space=pltpu.HBM)],
        out_specs=pl.BlockSpec(memory_space=pltpu.VMEM),
        out_shape=jax.ShapeDtypeStruct((len(PAIRS), BLOCK, BLOCK), jnp.float32),
        scratch_shapes=[
            pltpu.VMEM((parts, N1, STEP), jnp.float32),
            pltpu.VMEM((N1, N1), jnp.float32),
            pltpu.SemaphoreType.DMA((parts,)),
        ],
        compiler_params=pltpu.CompilerParams(vmem_limit_bytes=51 << 20),
    )(field)


def row_of(tile, k):
    return jnp.broadcast_to(tile[k : k + 1, :], TILE)


def lane_of(tile, k):
    return jnp.broadcast_to(tile[:, k : k + 1], TILE)


def inverse_factor(products, beside):
    tiles = PANEL // 8
    panels = RANK // PANEL
    row = lax.broadcasted_iota(jnp.int32, TILE, 0)
    lane = lax.broadcasted_iota(jnp.int32, TILE, 1)
    rows = [
        [products[PANEL * p + 8 * h : PANEL * p + 8 * h + 8, :] for h in range(tiles)] for p in range(panels)
    ]
    done = []
    for r in range(panels):
        first = PANEL * r
        last = r == panels - 1
        panel = rows[r] + ([] if last else rows[r + 1])
        height = len(panel)
        columns = [
            [lane_of(panel[h], first + k) if h >= k // 8 else None for h in range(height)]
            for k in range(PANEL)
        ]
        inside = (lane >= first) & (lane < first + PANEL)
        for h in range(height):
            unit = jnp.where(lane - (first + 8 * h) == row, 1.0, 0.0) if h < tiles else 0.0
            panel[h] = jnp.where(inside, unit, panel[h])
        scale = [None] * tiles
        pivot = row_of(columns[0][0], 0)
        for k in range(PANEL):
            g, at = divmod(k, 8)
            root = lax.rsqrt(pivot)
            scale[g] = root if at == 0 else jnp.where(row >= at, root, scale[g])
            if k == PANEL - 1 and last:
                break
            inverse = 1.0 / pivot
            if k < PANEL - 1:
                h, after = divmod(k + 1, 8)
                link = row_of(columns[k][h], after)
                pivot = row_of(columns[k + 1][h], after) - (link * link) * inverse
            below = [h for h in range(g, height) if not (h == g and at == 7)]
            factor = {
                h: (jnp.where(row > at, columns[k][h], 0.0) if h == g else columns[k][h]) * inverse
                for h in below
            }
            for j in range(k + 1, PANEL):
                across = row_of(columns[k][j // 8], j % 8)
                for h in below:
                    if h >= j // 8:
                        columns[j][h] = columns[j][h] - factor[h] * across
            across = row_of(panel[g], at)
            for h in below:
                panel[h] = panel[h] - factor[h] * across
        if not last:
            rows[r + 1] = panel[tiles:]
        panel = [panel[h] * scale[h] for h in range(tiles)]
        for h in range(tiles):
            done.append(jnp.where(lane < first + PANEL, panel[h], 0.0))
        beside(r)
        ahead = r + 2
        if ahead < panels:
            for h in range(tiles):
                update = None
                for i in range(8):
                    at = PANEL * ahead + 8 * h + i
                    term = sum(lane_of(panel[t], at) * panel[t] for t in range(tiles))
                    total = jnp.broadcast_to(jnp.sum(term, axis=0, keepdims=True), TILE)
                    update = total if i == 0 else jnp.where(row >= i, total, update)
                rows[ahead][h] = jnp.where(inside, 0.0, rows[ahead][h]) - update
        ahead = r + 3
        if ahead < panels:
            whole = jnp.concatenate(panel, axis=0)
            trail = exact_dot(whole[:, PANEL * ahead :], whole, ((0,), (0,)))
            for p in range(ahead, panels):
                for h in range(tiles):
                    at = PANEL * (p - ahead) + 8 * h
                    rows[p][h] = jnp.where(inside, 0.0, rows[p][h]) - trail[at : at + 8, :]
    return jnp.concatenate(done, axis=0)


def exact_dot(left, right, contract):
    return lax.dot_general(
        left, right, (contract, ((), ())), precision=HIGHEST, preferred_element_type=jnp.float32
    )


def split_three(values):
    high = values.astype(jnp.bfloat16)
    rest = values - high.astype(jnp.float32)
    middle = rest.astype(jnp.bfloat16)
    low = (rest - middle.astype(jnp.float32)).astype(jnp.bfloat16)
    return high, middle, low


def sweeps_kernel(
    core_ref,
    own_ref,
    other_ref,
    start_ref,
    field_ref,
    core_out_ref,
    basis_ref,
    gram_ref,
    wide_ref,
    image_ref,
    ahead_ref,
    parts_ref,
    results_ref,
    arrived,
    sent,
):
    nn, tn, nt = ((1,), (0,)), ((0,), (0,)), ((1,), (1,))
    variables, _, columns = field_ref.shape
    per = columns // STEP
    pieces = [(c // per, pl.ds((c % per) * STEP, STEP)) for c in range(variables * per)]
    fetches = [
        pltpu.make_async_copy(field_ref.at[v, :, span], parts_ref.at[c], arrived.at[c])
        for c, (v, span) in enumerate(pieces)
    ]
    for fetch in fetches:
        fetch.start()

    own_first = core_ref[0] == 0
    rows_half = own_ref.shape[0]
    for index, (i, j) in enumerate(PAIRS):
        at = (index * BLOCK) % rows_half
        own = own_ref[at : at + BLOCK, :]
        other = other_ref[at : at + BLOCK, :]
        block = jnp.where(own_first == (index * BLOCK < rows_half), own, other)
        for part, values in enumerate(split_three(block)):
            gram_ref[part, BLOCK * i : BLOCK * (i + 1), BLOCK * j : BLOCK * (j + 1)] = values
        if i != j:
            for part, values in enumerate(split_three(block.T)):
                gram_ref[part, BLOCK * j : BLOCK * (j + 1), BLOCK * i : BLOCK * (i + 1)] = values

    def widen(values):
        high, middle, low = split_three(values)
        wide_ref[:N1, :RANK] = high
        wide_ref[:N1, RANK:] = middle
        wide_ref[N1:, :RANK] = low

    def gram_times(at, size):
        span = pl.ds(at, size)
        wide = wide_ref[:N1, :]
        by_high = dot(gram_ref[0, span, :], wide, nn)
        by_middle = dot(gram_ref[1, span, :], wide, nn)
        small = dot(gram_ref[0, span, :], wide_ref[N1:, :RANK], nn) + dot(
            gram_ref[2, span, :], wide_ref[:N1, :RANK], nn
        )
        return by_high[:, :RANK] + (by_high[:, RANK:] + by_middle[:, :RANK] + (by_middle[:, RANK:] + small))

    widen(start_ref[...])
    image_ref[...] = gram_times(0, N1)

    def sweep(iteration, carry):
        image = image_ref[...]
        products = exact_dot(image, image, tn)
        widen(image)

        def beside(r):
            if r % 2 == 0:
                ahead_ref[64 * r : 64 * r + 128, :] = gram_times(64 * r, 128)

        inverse = inverse_factor(products, beside)
        image_ref[...] = exact_dot(ahead_ref[...], inverse, nt)
        return carry

    lax.fori_loop(0, ITERS - 1, sweep, 0)
    image = image_ref[...]
    products = exact_dot(image, image, tn)
    inverse = inverse_factor(products, lambda r: None)
    basis = exact_dot(image, inverse, nt)
    basis_ref[...] = basis
    basis_high, basis_low = split(basis)
    sends = [
        pltpu.make_async_copy(results_ref.at[c], core_out_ref.at[v, :, span], sent.at[c])
        for c, (v, span) in enumerate(pieces)
    ]
    for c in range(len(pieces)):
        fetches[c].wait()
        high, low = split(parts_ref[c])
        results_ref[c] = dot(basis_high, high, tn) + (dot(basis_high, low, tn) + dot(basis_low, high, tn))
        sends[c].start()
    for send in sends:
        send.wait()


def sweeps(core, own, other, start_basis, field):
    variables, _, columns = field.shape
    parts = variables * columns // STEP
    whole = pl.BlockSpec(memory_space=pltpu.VMEM)
    anywhere = pl.BlockSpec(memory_space=pltpu.HBM)
    return pl.pallas_call(
        sweeps_kernel,
        in_specs=[pl.BlockSpec(memory_space=pltpu.SMEM), whole, whole, whole, anywhere],
        out_specs=[anywhere, whole],
        out_shape=[
            jax.ShapeDtypeStruct((variables, RANK, columns), jnp.float32),
            jax.ShapeDtypeStruct((N1, RANK), jnp.float32),
        ],
        scratch_shapes=[
            pltpu.VMEM((3, N1, N1), jnp.bfloat16),
            pltpu.VMEM((2 * N1, 2 * RANK), jnp.bfloat16),
            pltpu.VMEM((N1, RANK), jnp.float32),
            pltpu.VMEM((N1, RANK), jnp.float32),
            pltpu.VMEM((parts, N1, STEP), jnp.float32),
            pltpu.VMEM((parts, RANK, STEP), jnp.float32),
            pltpu.SemaphoreType.DMA((parts,)),
            pltpu.SemaphoreType.DMA((parts,)),
        ],
        compiler_params=pltpu.CompilerParams(vmem_limit_bytes=51 << 20),
    )(core, own, other, start_basis, field)


def spread(block, axes, size):
    return lax.all_to_all(jnp.broadcast_to(block, (size,) + block.shape), axes, 0, 0)


def all_sum(packed):
    core = lax.axis_index("core")
    half = packed.shape[0] // 2
    swap = [(0, 1), (1, 0)]
    mine = lax.dynamic_slice_in_dim(packed, core * half, half)
    theirs = lax.dynamic_slice_in_dim(packed, (1 - core) * half, half)
    own = mine + lax.ppermute(theirs, "core", swap)
    plane = lax.axis_size("y") * lax.axis_size("x")
    piece = half // plane
    pieces = lax.all_to_all(own.reshape(plane, piece, BLOCK), ("y", "x"), 0, 0)
    own = jnp.sum(pieces, axis=0)
    own = jnp.sum(spread(own, "z", lax.axis_size("z")), axis=0)
    own = spread(own, ("y", "x"), plane).reshape(half, BLOCK)
    return core, own, lax.ppermute(own, "core", swap)


def local(tensor_field, start_basis):
    packed = partial_gram(tensor_field).reshape(len(PAIRS) * BLOCK, BLOCK)
    core, own, other = all_sum(packed)
    return tuple(sweeps(core.astype(jnp.int32).reshape(1), own, other, start_basis, tensor_field))


def solution(mesh):
    fine = Mesh(mesh.devices.reshape(8, 4, 4, 2), ("z", "y", "x", "core"))
    spec = P(("x", "core"), None, ("z", "y"))
    return jax.shard_map(local, mesh=fine, in_specs=(spec, P()), out_specs=(spec, P()), check_vma=False)
```

time: 397 us -> 73.6 us (0.19)
  waiting for transfers between devices: 258 us -> 2.51 us
  other arithmetic: 91.7 us -> 0.07 us
  blocking collectives: 0 us -> 40.9 us
  matrix products: 26.9 us -> 0 us
  Pallas kernels: 0 us -> 22 us
  between operations: 14.7 us -> 0.69 us
  starting transfers between devices: 0.04 us -> 7.22 us
    psum x1 -> x0, waiting for transfers between devices: 258 us -> none  [local(): gram_full = lax.psum(partial_gram, ('grid', 'var'))]
    another operation x20 -> x0, other arithmetic: 91.6 us -> none  [the longest x12 49.7 us: orthonormal(): factor = jnp.linalg.cholesky(products)]
    all_to_all x0 -> x3, blocking collectives: none -> 40.9 us  [the longest x2 27.2 us: spread(): lax.all_to_all(jnp.broadcast_to(block, (size,) + block.shape), axes, 0, 0)]
    dot_general x10 -> x0, matrix products: 25.2 us -> none  [the longest x1 10.6 us: local(): lax.dot_general(tensor_field, tensor_field, (((0, 2), (0, 2)), ((), ())),...]
    pallas_call x0 -> x2, Pallas kernels: none -> 22 us  [the longest x1 17.9 us: sweeps(): pl.pallas_call(sweeps_kernel, in_specs=[pl.BlockSpec(memory_space=pltpu.S...]
    ppermute x0 -> x2, starting transfers between devices: none -> 7.22 us  [the longest x1 3.9 us: all_sum(): return (core, own, lax.ppermute(own, 'core', swap))]
  transfers between devices with their start and end apart: 1 -> 2, of which waited for: 1 -> 2; matrix products, arithmetic and copies ran while one was open for 0% -> 0% of each run, Pallas kernels for 0% -> 0%
where the time goes in v2:
time: 73.6 us; the launch traced here: 73.4 us
  blocking collectives  40.9 us (56%)
  Pallas kernels  22 us (30%)
  starting transfers between devices  7.22 us (10%)
  waiting for transfers between devices  2.51 us (3%)
    all_to_all x2, blocking collectives, spread(): lax.all_to_all(jnp.broadcast_to(block, (size,) + block.shape), axes, 0, 0)  27.2 us
    pallas_call x1, Pallas kernels, sweeps(): pl.pallas_call(sweeps_kernel, in_specs=[pl.BlockSpec(memory_space=pltpu.S...  17.9 us
    all_to_all x1, blocking collectives, all_sum(): pieces = lax.all_to_all(own.reshape(plane, piece, BLOCK), ('y', 'x'), 0, 0)  13.6 us
    pallas_call x1, Pallas kernels, partial_gram(): pl.pallas_call(gram_kernel, in_specs=[pl.BlockSpec(memory_space=pltpu.HBM...  4.11 us
    ppermute x1, starting transfers between devices, all_sum(): return (core, own, lax.ppermute(own, 'core', swap))  3.9 us
    ppermute x1, starting transfers between devices, all_sum(): own = mine + lax.ppermute(theirs, 'core', swap)  3.32 us
  transfers between devices with their start and end apart: 2, of which 2 were waited for; matrix products, arithmetic and copies ran while one was open for 0% of the time, Pallas kernels for 0%

profile of v2, /device:TPU:1, one launch (start us, length us, event | category | flops | bytes accessed | tf_op | source)
XLA Modules:
  0.0 73.4 jit_solution(5899801521853425106)
XLA Ops:
  0.6 0.0 copy-start
  0.6 4.1 %shard_map.41 = f32[10,128,128]{2,1,0:T(8,128)S(1)} custom-call(f32[2,512,1024]{2,1,0:T(8,128)} %field_ref.3), custom_call_target="tpu_custom_call" | custom-call | tf_op jit(solution)/shard_map/pallas_call | solution.py:60
  4.8 3.3 %collective-permute-start = (f32[640,128]{1,0:T(8,128)S(1)}, f32[640,128]{1,0:T(8,128)S(1)}, u32[]{:S(2)}, u32[]{:S(2)}) collective-permute-start(f32[640,128]{1,0:T(8,128)S(1)} %constant_dynamic-slice_fusion), channel_id=1, source_target_pairs={{0,1},{1,0},{2,3},{3,2},{4,5},{5,4},{6,7},{7,6},{8,9},{9,8},{10,11... | collective-permute-start | bytes 983048 | tf_op jit(solution)/shard_map/ppermute | solution.py:301
  8.1 1.3 %collective-permute-done = f32[640,128]{1,0:T(8,128)S(1)} collective-permute-done((f32[640,128]{1,0:T(8,128)S(1)}, f32[640,128]{1,0:T(8,128)S(1)}, u32[]{:S(2)}, u32[]{:S(2)}) %collective-permute-start) | collective-permute-done | bytes 327712 | tf_op jit(solution)/shard_map/ppermute | solution.py:301
  9.4 13.6 %all_to_all.15 = f32[16,40,128]{2,1,0:T(8,128)S(1)} all-to-all(f32[16,40,128]{2,1,0:T(8,128)S(1)} %bitcast.8), channel_id=1, replica_groups=mesh['z'=8,'y'=4,'x'=4,'core'=2] {'y','x'}, dimensions={0} | all-to-all | bytes 655360 | tf_op jit(solution)/shard_map/all_to_all | solution.py:304
  23.1 16.3 %all_to_all.16 = f32[8,40,128]{2,1,0:T(8,128)S(1)} all-to-all(f32[8,40,128]{2,1,0:T(8,128)S(1)} %broadcast_in_dim.6), channel_id=1, replica_groups=mesh['z'=8,'y'=4,'x'=4,'core'=2] {'z'}, dimensions={0} | all-to-all | bytes 327680 | tf_op jit(solution)/shard_map/all_to_all | solution.py:292
  39.4 10.9 %all_to_all.17 = f32[16,40,128]{2,1,0:T(8,128)S(1)} all-to-all(f32[16,40,128]{2,1,0:T(8,128)S(1)} %broadcast_in_dim.7), channel_id=1, replica_groups=mesh['z'=8,'y'=4,'x'=4,'core'=2] {'y','x'}, dimensions={0} | all-to-all | bytes 655360 | tf_op jit(solution)/shard_map/all_to_all | solution.py:292
  50.4 3.9 %collective-permute-start.1 = (f32[640,128]{1,0:T(8,128)S(1)}, f32[640,128]{1,0:T(8,128)S(1)}, u32[]{:S(2)}, u32[]{:S(2)}) collective-permute-start(f32[640,128]{1,0:T(8,128)S(1)} %bitcast.6), channel_id=1, source_target_pairs={{0,1},{1,0},{2,3},{3,2},{4,5},{5,4},{6,7},{7,6},{8,9},{9,8},{10,11... | collective-permute-start | bytes 983048 | tf_op jit(solution)/shard_map/ppermute | solution.py:308
  54.3 1.3 %collective-permute-done.1.other_ref = f32[640,128]{1,0:T(8,128)S(1)} collective-permute-done((f32[640,128]{1,0:T(8,128)S(1)}, f32[640,128]{1,0:T(8,128)S(1)}, u32[]{:S(2)}, u32[]{:S(2)}) %collective-permute-start.1) | collective-permute-done | bytes 327712 | tf_op jit(solution)/shard_map/ppermute | solution.py:308
  55.5 0.0 copy-done
  55.5 17.9 %shard_map.42 = (f32[2,128,1024]{2,1,0:T(8,128)}, f32[512,128]{1,0:T(8,128)}) custom-call(s32[1]{0:T(128)} %bitcast.core_ref, f32[640,128]{1,0:T(8,128)S(1)} %bitcast.7, f32[640,128]{1,0:T(8,128)S(1)} %collective-permute-done.1.other_ref, f32[512,128]{1,0:T(8,128)S(1)} %copy-done, f32[2,512,1024]{2,1,0:T(8,128)} %field_ref.3), custom_call_target="tpu_custom_call" | custom-call | tf_op jit(solution)/shard_map/pallas_call | solution.py:269
  (6 shorter events, 0.1 us)
Async XLA Ops:
  0.6 54.9 %copy-start = (f32[512,128]{1,0:T(8,128)S(1)}, f32[512,128]{1,0:T(8,128)}, u32[]{:S(2)}) copy-start(f32[512,128]{1,0:T(8,128)} %start_ref.1) | copy-start | bytes 786436
  4.8 4.6 %collective-permute-start = (f32[640,128]{1,0:T(8,128)S(1)}, f32[640,128]{1,0:T(8,128)S(1)}, u32[]{:S(2)}, u32[]{:S(2)}) collective-permute-start(f32[640,128]{1,0:T(8,128)S(1)} %constant_dynamic-slice_fusion), channel_id=1, source_target_pairs={{0,1},{1,0},{2,3},{3,2},{4,5},{5,4},{6,7},{7,6},{8,9},{9,8},{10,11... | collective-permute-start | bytes 983048 | tf_op jit(solution)/shard_map/ppermute | solution.py:301
  50.4 5.2 %collective-permute-start.1 = (f32[640,128]{1,0:T(8,128)S(1)}, f32[640,128]{1,0:T(8,128)S(1)}, u32[]{:S(2)}, u32[]{:S(2)}) collective-permute-start(f32[640,128]{1,0:T(8,128)S(1)} %bitcast.6), channel_id=1, source_target_pairs={{0,1},{1,0},{2,3},{3,2},{4,5},{5,4},{6,7},{7,6},{8,9},{9,8},{10,11... | collective-permute-start | bytes 983048 | tf_op jit(solution)/shard_map/ppermute | solution.py:308

commit v3 on v2

--- a/solution.py
+++ b/solution.py
@@ -177,15 +177,16 @@
     core_out_ref,
     basis_ref,
     gram_ref,
-    wide_ref,
     image_ref,
     ahead_ref,
     parts_ref,
+    high_ref,
+    low_ref,
     results_ref,
     arrived,
     sent,
 ):
-    nn, tn, nt = ((1,), (0,)), ((0,), (0,)), ((1,), (1,))
+    nn, nt = ((1,), (0,)), ((1,), (1,))
     variables, _, columns = field_ref.shape
     per = columns // STEP
     pieces = [(c // per, pl.ds((c % per) * STEP, STEP)) for c in range(variables * per)]
@@ -209,53 +210,62 @@
             for part, values in enumerate(split_three(block.T)):
                 gram_ref[part, BLOCK * j : BLOCK * (j + 1), BLOCK * i : BLOCK * (i + 1)] = values
 
-    def widen(values):
-        high, middle, low = split_three(values)
-        wide_ref[:N1, :RANK] = high
-        wide_ref[:N1, RANK:] = middle
-        wide_ref[N1:, :RANK] = low
-
-    def gram_times(at, size):
+    def keep(ref, values, at=0):
+        for part, piece in enumerate(split_three(values)):
+            ref[RANK * part : RANK * (part + 1), at : at + values.shape[1]] = piece
+
+    def times_gram(at, size):
         span = pl.ds(at, size)
-        wide = wide_ref[:N1, :]
-        by_high = dot(gram_ref[0, span, :], wide, nn)
-        by_middle = dot(gram_ref[1, span, :], wide, nn)
-        small = dot(gram_ref[0, span, :], wide_ref[N1:, :RANK], nn) + dot(
-            gram_ref[2, span, :], wide_ref[:N1, :RANK], nn
-        )
-        return by_high[:, :RANK] + (by_high[:, RANK:] + by_middle[:, :RANK] + (by_middle[:, RANK:] + small))
-
-    widen(start_ref[...])
-    image_ref[...] = gram_times(0, N1)
+        by_high = dot(image_ref[...], gram_ref[0, :, span], nn)
+        by_middle = dot(image_ref[: 2 * RANK, :], gram_ref[1, :, span], nn)
+        by_low = dot(image_ref[:RANK, :], gram_ref[2, :, span], nn)
+        small = by_middle[RANK:] + (by_high[2 * RANK :] + by_low)
+        return by_high[:RANK] + (by_high[RANK : 2 * RANK] + by_middle[:RANK] + small)
+
+    def products():
+        both = dot(image_ref[...], image_ref[: 2 * RANK, :], nt)
+        small = both[2 * RANK :, :RANK] + dot(image_ref[:RANK, :], image_ref[2 * RANK :, :], nt)
+        middle = both[:RANK, RANK:] + both[RANK : 2 * RANK, :RANK]
+        return both[:RANK, :RANK] + (middle + (both[RANK : 2 * RANK, RANK:] + small))
+
+    def times_inverse(inverse, ref):
+        high, middle, low = split_three(inverse)
+        left = jnp.concatenate([high, low, middle, middle, high, high], axis=1)
+        by_high, by_middle, by_low = (ref[RANK * part : RANK * (part + 1), :] for part in range(3))
+        right = jnp.concatenate([by_low, by_high, by_middle, by_high, by_middle, by_high], axis=0)
+        return dot(left, right, nn)
+
+    keep(image_ref, start_ref[...].T)
+    keep(image_ref, times_gram(0, N1))
 
     def sweep(iteration, carry):
-        image = image_ref[...]
-        products = exact_dot(image, image, tn)
-        widen(image)
-
         def beside(r):
-            if r % 2 == 0:
-                ahead_ref[64 * r : 64 * r + 128, :] = gram_times(64 * r, 128)
-
-        inverse = inverse_factor(products, beside)
-        image_ref[...] = exact_dot(ahead_ref[...], inverse, nt)
+            if r in (0, 2):
+                keep(ahead_ref, times_gram(128 * r, 256), 128 * r)
+
+        inverse = inverse_factor(products(), beside)
+        keep(image_ref, times_inverse(inverse, ahead_ref))
         return carry
 
     lax.fori_loop(0, ITERS - 1, sweep, 0)
-    image = image_ref[...]
-    products = exact_dot(image, image, tn)
-    inverse = inverse_factor(products, lambda r: None)
-    basis = exact_dot(image, inverse, nt)
-    basis_ref[...] = basis
+
+    def beside(r):
+        if r < len(pieces):
+            fetches[r].wait()
+            high_ref[r], low_ref[r] = split(parts_ref[r])
+
+    inverse = inverse_factor(products(), beside)
+    basis = times_inverse(inverse, image_ref)
+    basis_ref[...] = basis.T
     basis_high, basis_low = split(basis)
+    basis_parts = jnp.concatenate([basis_high, basis_low], axis=0)
     sends = [
         pltpu.make_async_copy(results_ref.at[c], core_out_ref.at[v, :, span], sent.at[c])
         for c, (v, span) in enumerate(pieces)
     ]
     for c in range(len(pieces)):
-        fetches[c].wait()
-        high, low = split(parts_ref[c])
-        results_ref[c] = dot(basis_high, high, tn) + (dot(basis_high, low, tn) + dot(basis_low, high, tn))
+        by_high = dot(basis_parts, high_ref[c], nn)
+        results_ref[c] = by_high[:RANK] + (by_high[RANK:] + dot(basis_high, low_ref[c], nn))
         sends[c].start()
     for send in sends:
         send.wait()
@@ -276,10 +286,11 @@
         ],
         scratch_shapes=[
             pltpu.VMEM((3, N1, N1), jnp.bfloat16),
-            pltpu.VMEM((2 * N1, 2 * RANK), jnp.bfloat16),
-            pltpu.VMEM((N1, RANK), jnp.float32),
-            pltpu.VMEM((N1, RANK), jnp.float32),
+            pltpu.VMEM((3 * RANK, N1), jnp.bfloat16),
+            pltpu.VMEM((3 * RANK, N1), jnp.bfloat16),
             pltpu.VMEM((parts, N1, STEP), jnp.float32),
+            pltpu.VMEM((parts, N1, STEP), jnp.bfloat16),
+            pltpu.VMEM((parts, N1, STEP), jnp.bfloat16),
             pltpu.VMEM((parts, RANK, STEP), jnp.float32),
             pltpu.SemaphoreType.DMA((parts,)),
             pltpu.SemaphoreType.DMA((parts,)),

time: 73.6 us -> 72.6 us (0.986)
  Pallas kernels: 22 us -> 21 us
    pallas_call x1, Pallas kernels: 17.9 us -> 16.9 us  [sweeps(): pl.pallas_call(sweeps_kernel, in_specs=[pl.BlockSpec(memory_space=pltpu.S...]
where the time goes in v3:
time: 72.6 us; the launch traced here: 72.4 us
  blocking collectives  40.9 us (56%)
  Pallas kernels  21 us (29%)
  starting transfers between devices  7.22 us (10%)
  waiting for transfers between devices  2.51 us (3%)
    all_to_all x2, blocking collectives, spread(): lax.all_to_all(jnp.broadcast_to(block, (size,) + block.shape), axes, 0, 0)  27.2 us
    pallas_call x1, Pallas kernels, sweeps(): pl.pallas_call(sweeps_kernel, in_specs=[pl.BlockSpec(memory_space=pltpu.S...  16.9 us
    all_to_all x1, blocking collectives, all_sum(): pieces = lax.all_to_all(own.reshape(plane, piece, BLOCK), ('y', 'x'), 0, 0)  13.6 us
    pallas_call x1, Pallas kernels, partial_gram(): pl.pallas_call(gram_kernel, in_specs=[pl.BlockSpec(memory_space=pltpu.HBM...  4.11 us
    ppermute x1, starting transfers between devices, all_sum(): return (core, own, lax.ppermute(own, 'core', swap))  3.9 us
    ppermute x1, starting transfers between devices, all_sum(): own = mine + lax.ppermute(theirs, 'core', swap)  3.32 us
  transfers between devices with their start and end apart: 2, of which 2 were waited for; matrix products, arithmetic and copies ran while one was open for 0% of the time, Pallas kernels for 0%

profile of v3, /device:TPU:1, one launch (start us, length us, event | category | flops | bytes accessed | tf_op | source)
XLA Modules:
  0.0 72.4 jit_solution(6923442625658718183)
XLA Ops:
  0.6 0.0 copy-start
  0.6 4.1 %shard_map.41 = f32[10,128,128]{2,1,0:T(8,128)S(1)} custom-call(f32[2,512,1024]{2,1,0:T(8,128)} %field_ref.3), custom_call_target="tpu_custom_call" | custom-call | tf_op jit(solution)/shard_map/pallas_call | solution.py:60
  4.8 3.3 %collective-permute-start = (f32[640,128]{1,0:T(8,128)S(1)}, f32[640,128]{1,0:T(8,128)S(1)}, u32[]{:S(2)}, u32[]{:S(2)}) collective-permute-start(f32[640,128]{1,0:T(8,128)S(1)} %constant_dynamic-slice_fusion), channel_id=1, source_target_pairs={{0,1},{1,0},{2,3},{3,2},{4,5},{5,4},{6,7},{7,6},{8,9},{9,8},{10,11... | collective-permute-start | bytes 983048 | tf_op jit(solution)/shard_map/ppermute | solution.py:312
  8.1 1.3 %collective-permute-done = f32[640,128]{1,0:T(8,128)S(1)} collective-permute-done((f32[640,128]{1,0:T(8,128)S(1)}, f32[640,128]{1,0:T(8,128)S(1)}, u32[]{:S(2)}, u32[]{:S(2)}) %collective-permute-start) | collective-permute-done | bytes 327712 | tf_op jit(solution)/shard_map/ppermute | solution.py:312
  9.4 13.6 %all_to_all.15 = f32[16,40,128]{2,1,0:T(8,128)S(1)} all-to-all(f32[16,40,128]{2,1,0:T(8,128)S(1)} %bitcast.8), channel_id=1, replica_groups=mesh['z'=8,'y'=4,'x'=4,'core'=2] {'y','x'}, dimensions={0} | all-to-all | bytes 655360 | tf_op jit(solution)/shard_map/all_to_all | solution.py:315
  23.1 16.3 %all_to_all.16 = f32[8,40,128]{2,1,0:T(8,128)S(1)} all-to-all(f32[8,40,128]{2,1,0:T(8,128)S(1)} %broadcast_in_dim.6), channel_id=1, replica_groups=mesh['z'=8,'y'=4,'x'=4,'core'=2] {'z'}, dimensions={0} | all-to-all | bytes 327680 | tf_op jit(solution)/shard_map/all_to_all | solution.py:303
  39.4 10.9 %all_to_all.17 = f32[16,40,128]{2,1,0:T(8,128)S(1)} all-to-all(f32[16,40,128]{2,1,0:T(8,128)S(1)} %broadcast_in_dim.7), channel_id=1, replica_groups=mesh['z'=8,'y'=4,'x'=4,'core'=2] {'y','x'}, dimensions={0} | all-to-all | bytes 655360 | tf_op jit(solution)/shard_map/all_to_all | solution.py:303
  50.4 3.9 %collective-permute-start.1 = (f32[640,128]{1,0:T(8,128)S(1)}, f32[640,128]{1,0:T(8,128)S(1)}, u32[]{:S(2)}, u32[]{:S(2)}) collective-permute-start(f32[640,128]{1,0:T(8,128)S(1)} %bitcast.6), channel_id=1, source_target_pairs={{0,1},{1,0},{2,3},{3,2},{4,5},{5,4},{6,7},{7,6},{8,9},{9,8},{10,11... | collective-permute-start | bytes 983048 | tf_op jit(solution)/shard_map/ppermute | solution.py:319
  54.3 1.3 %collective-permute-done.1.other_ref = f32[640,128]{1,0:T(8,128)S(1)} collective-permute-done((f32[640,128]{1,0:T(8,128)S(1)}, f32[640,128]{1,0:T(8,128)S(1)}, u32[]{:S(2)}, u32[]{:S(2)}) %collective-permute-start.1) | collective-permute-done | bytes 327712 | tf_op jit(solution)/shard_map/ppermute | solution.py:319
  55.5 0.0 copy-done
  55.5 16.9 %shard_map.42 = (f32[2,128,1024]{2,1,0:T(8,128)}, f32[512,128]{1,0:T(8,128)}) custom-call(s32[1]{0:T(128)} %bitcast.core_ref, f32[640,128]{1,0:T(8,128)S(1)} %bitcast.7, f32[640,128]{1,0:T(8,128)S(1)} %collective-permute-done.1.other_ref, f32[512,128]{1,0:T(8,128)S(1)} %copy-done, f32[2,512,1024]{2,1,0:T(8,128)} %field_ref.3), custom_call_target="tpu_custom_call" | custom-call | tf_op jit(solution)/shard_map/pallas_call | solution.py:279
  (6 shorter events, 0.1 us)
Async XLA Ops:
  0.6 54.9 %copy-start = (f32[512,128]{1,0:T(8,128)S(1)}, f32[512,128]{1,0:T(8,128)}, u32[]{:S(2)}) copy-start(f32[512,128]{1,0:T(8,128)} %start_ref.1) | copy-start | bytes 786436
  4.8 4.6 %collective-permute-start = (f32[640,128]{1,0:T(8,128)S(1)}, f32[640,128]{1,0:T(8,128)S(1)}, u32[]{:S(2)}, u32[]{:S(2)}) collective-permute-start(f32[640,128]{1,0:T(8,128)S(1)} %constant_dynamic-slice_fusion), channel_id=1, source_target_pairs={{0,1},{1,0},{2,3},{3,2},{4,5},{5,4},{6,7},{7,6},{8,9},{9,8},{10,11... | collective-permute-start | bytes 983048 | tf_op jit(solution)/shard_map/ppermute | solution.py:312
  50.4 5.2 %collective-permute-start.1 = (f32[640,128]{1,0:T(8,128)S(1)}, f32[640,128]{1,0:T(8,128)S(1)}, u32[]{:S(2)}, u32[]{:S(2)}) collective-permute-start(f32[640,128]{1,0:T(8,128)S(1)} %bitcast.6), channel_id=1, source_target_pairs={{0,1},{1,0},{2,3},{3,2},{4,5},{5,4},{6,7},{7,6},{8,9},{9,8},{10,11... | collective-permute-start | bytes 983048 | tf_op jit(solution)/shard_map/ppermute | solution.py:319

commit v4 on v3

--- a/solution.py
+++ b/solution.py
@@ -11,7 +11,6 @@
 PANEL = 16
 BLOCK = 128
 PAIRS = [(i, j) for i in range(N1 // BLOCK) for j in range(i, N1 // BLOCK)]
-HIGHEST = lax.Precision.HIGHEST
 STEP = 512
 TILE = (8, 128)
 
@@ -135,29 +134,15 @@
         beside(r)
         ahead = r + 2
         if ahead < panels:
-            for h in range(tiles):
-                update = None
-                for i in range(8):
-                    at = PANEL * ahead + 8 * h + i
-                    term = sum(lane_of(panel[t], at) * panel[t] for t in range(tiles))
-                    total = jnp.broadcast_to(jnp.sum(term, axis=0, keepdims=True), TILE)
-                    update = total if i == 0 else jnp.where(row >= i, total, update)
-                rows[ahead][h] = jnp.where(inside, 0.0, rows[ahead][h]) - update
-        ahead = r + 3
-        if ahead < panels:
-            whole = jnp.concatenate(panel, axis=0)
-            trail = exact_dot(whole[:, PANEL * ahead :], whole, ((0,), (0,)))
+            high, middle, low = split_three(jnp.concatenate(panel, axis=0))
+            left = jnp.concatenate([high, low, middle, middle, high, high], axis=0)
+            right = jnp.concatenate([low, high, middle, high, middle, high], axis=0)
+            trail = dot(left, right, ((0,), (0,)))
             for p in range(ahead, panels):
                 for h in range(tiles):
-                    at = PANEL * (p - ahead) + 8 * h
+                    at = PANEL * p + 8 * h
                     rows[p][h] = jnp.where(inside, 0.0, rows[p][h]) - trail[at : at + 8, :]
     return jnp.concatenate(done, axis=0)
-
-
-def exact_dot(left, right, contract):
-    return lax.dot_general(
-        left, right, (contract, ((), ())), precision=HIGHEST, preferred_element_type=jnp.float32
-    )
 
 
 def split_three(values):
@@ -183,8 +168,10 @@
     high_ref,
     low_ref,
     results_ref,
+    result_ref,
     arrived,
     sent,
+    basis_sent,
 ):
     nn, nt = ((1,), (0,)), ((1,), (1,))
     variables, _, columns = field_ref.shape
@@ -249,14 +236,18 @@
 
     lax.fori_loop(0, ITERS - 1, sweep, 0)
 
+    for fetch in fetches:
+        fetch.wait()
+
     def beside(r):
         if r < len(pieces):
-            fetches[r].wait()
             high_ref[r], low_ref[r] = split(parts_ref[r])
 
     inverse = inverse_factor(products(), beside)
     basis = times_inverse(inverse, image_ref)
-    basis_ref[...] = basis.T
+    result_ref[...] = basis.T
+    basis_send = pltpu.make_async_copy(result_ref, basis_ref, basis_sent)
+    basis_send.start()
     basis_high, basis_low = split(basis)
     basis_parts = jnp.concatenate([basis_high, basis_low], axis=0)
     sends = [
@@ -267,6 +258,7 @@
         by_high = dot(basis_parts, high_ref[c], nn)
         results_ref[c] = by_high[:RANK] + (by_high[RANK:] + dot(basis_high, low_ref[c], nn))
         sends[c].start()
+    basis_send.wait()
     for send in sends:
         send.wait()
 
@@ -279,7 +271,7 @@
     return pl.pallas_call(
         sweeps_kernel,
         in_specs=[pl.BlockSpec(memory_space=pltpu.SMEM), whole, whole, whole, anywhere],
-        out_specs=[anywhere, whole],
+        out_specs=[anywhere, anywhere],
         out_shape=[
             jax.ShapeDtypeStruct((variables, RANK, columns), jnp.float32),
             jax.ShapeDtypeStruct((N1, RANK), jnp.float32),
@@ -292,8 +284,10 @@
             pltpu.VMEM((parts, N1, STEP), jnp.bfloat16),
             pltpu.VMEM((parts, N1, STEP), jnp.bfloat16),
             pltpu.VMEM((parts, RANK, STEP), jnp.float32),
+            pltpu.VMEM((N1, RANK), jnp.float32),
             pltpu.SemaphoreType.DMA((parts,)),
             pltpu.SemaphoreType.DMA((parts,)),
+            pltpu.SemaphoreType.DMA,
         ],
         compiler_params=pltpu.CompilerParams(vmem_limit_bytes=51 << 20),
     )(core, own, other, start_basis, field)

time: 72.6 us -> 70.6 us (0.972)
  Pallas kernels: 21 us -> 19 us
    pallas_call x1, Pallas kernels: 16.9 us -> 14.9 us  [sweeps(): pl.pallas_call(sweeps_kernel, in_specs=[pl.BlockSpec(memory_space=pltpu.S...]
where the time goes in v4:
time: 70.6 us; the launch traced here: 70.4 us
  blocking collectives  40.9 us (58%)
  Pallas kernels  19 us (27%)
  starting transfers between devices  7.22 us (10%)
  waiting for transfers between devices  2.51 us (4%)
    all_to_all x2, blocking collectives, spread(): lax.all_to_all(jnp.broadcast_to(block, (size,) + block.shape), axes, 0, 0)  27.2 us
    pallas_call x1, Pallas kernels, sweeps(): pl.pallas_call(sweeps_kernel, in_specs=[pl.BlockSpec(memory_space=pltpu.S...  14.9 us
    all_to_all x1, blocking collectives, all_sum(): pieces = lax.all_to_all(own.reshape(plane, piece, BLOCK), ('y', 'x'), 0, 0)  13.6 us
    pallas_call x1, Pallas kernels, partial_gram(): pl.pallas_call(gram_kernel, in_specs=[pl.BlockSpec(memory_space=pltpu.HBM...  4.11 us
    ppermute x1, starting transfers between devices, all_sum(): return (core, own, lax.ppermute(own, 'core', swap))  3.9 us
    ppermute x1, starting transfers between devices, all_sum(): own = mine + lax.ppermute(theirs, 'core', swap)  3.32 us
  transfers between devices with their start and end apart: 2, of which 2 were waited for; matrix products, arithmetic and copies ran while one was open for 0% of the time, Pallas kernels for 0%

profile of v4, /device:TPU:1, one launch (start us, length us, event | category | flops | bytes accessed | tf_op | source)
XLA Modules:
  0.0 70.4 jit_solution(15404866530274392543)
XLA Ops:
  0.6 0.0 copy-start
  0.6 4.1 %shard_map.41 = f32[10,128,128]{2,1,0:T(8,128)S(1)} custom-call(f32[2,512,1024]{2,1,0:T(8,128)} %field_ref.3), custom_call_target="tpu_custom_call" | custom-call | tf_op jit(solution)/shard_map/pallas_call | solution.py:59
  4.8 3.3 %collective-permute-start = (f32[640,128]{1,0:T(8,128)S(1)}, f32[640,128]{1,0:T(8,128)S(1)}, u32[]{:S(2)}, u32[]{:S(2)}) collective-permute-start(f32[640,128]{1,0:T(8,128)S(1)} %constant_dynamic-slice_fusion), channel_id=1, source_target_pairs={{0,1},{1,0},{2,3},{3,2},{4,5},{5,4},{6,7},{7,6},{8,9},{9,8},{10,11... | collective-permute-start | bytes 983048 | tf_op jit(solution)/shard_map/ppermute | solution.py:306
  8.1 1.3 %collective-permute-done = f32[640,128]{1,0:T(8,128)S(1)} collective-permute-done((f32[640,128]{1,0:T(8,128)S(1)}, f32[640,128]{1,0:T(8,128)S(1)}, u32[]{:S(2)}, u32[]{:S(2)}) %collective-permute-start) | collective-permute-done | bytes 327712 | tf_op jit(solution)/shard_map/ppermute | solution.py:306
  9.4 13.6 %all_to_all.15 = f32[16,40,128]{2,1,0:T(8,128)S(1)} all-to-all(f32[16,40,128]{2,1,0:T(8,128)S(1)} %bitcast.8), channel_id=1, replica_groups=mesh['z'=8,'y'=4,'x'=4,'core'=2] {'y','x'}, dimensions={0} | all-to-all | bytes 655360 | tf_op jit(solution)/shard_map/all_to_all | solution.py:309
  23.1 16.3 %all_to_all.16 = f32[8,40,128]{2,1,0:T(8,128)S(1)} all-to-all(f32[8,40,128]{2,1,0:T(8,128)S(1)} %broadcast_in_dim.6), channel_id=1, replica_groups=mesh['z'=8,'y'=4,'x'=4,'core'=2] {'z'}, dimensions={0} | all-to-all | bytes 327680 | tf_op jit(solution)/shard_map/all_to_all | solution.py:297
  39.4 10.9 %all_to_all.17 = f32[16,40,128]{2,1,0:T(8,128)S(1)} all-to-all(f32[16,40,128]{2,1,0:T(8,128)S(1)} %broadcast_in_dim.7), channel_id=1, replica_groups=mesh['z'=8,'y'=4,'x'=4,'core'=2] {'y','x'}, dimensions={0} | all-to-all | bytes 655360 | tf_op jit(solution)/shard_map/all_to_all | solution.py:297
  50.4 3.9 %collective-permute-start.1 = (f32[640,128]{1,0:T(8,128)S(1)}, f32[640,128]{1,0:T(8,128)S(1)}, u32[]{:S(2)}, u32[]{:S(2)}) collective-permute-start(f32[640,128]{1,0:T(8,128)S(1)} %bitcast.6), channel_id=1, source_target_pairs={{0,1},{1,0},{2,3},{3,2},{4,5},{5,4},{6,7},{7,6},{8,9},{9,8},{10,11... | collective-permute-start | bytes 983048 | tf_op jit(solution)/shard_map/ppermute | solution.py:313
  54.3 1.3 %collective-permute-done.1.other_ref = f32[640,128]{1,0:T(8,128)S(1)} collective-permute-done((f32[640,128]{1,0:T(8,128)S(1)}, f32[640,128]{1,0:T(8,128)S(1)}, u32[]{:S(2)}, u32[]{:S(2)}) %collective-permute-start.1) | collective-permute-done | bytes 327712 | tf_op jit(solution)/shard_map/ppermute | solution.py:313
  55.5 0.0 copy-done
  55.5 14.9 %shard_map.42 = (f32[2,128,1024]{2,1,0:T(8,128)}, f32[512,128]{1,0:T(8,128)}) custom-call(s32[1]{0:T(128)} %bitcast.core_ref, f32[640,128]{1,0:T(8,128)S(1)} %bitcast.7, f32[640,128]{1,0:T(8,128)S(1)} %collective-permute-done.1.other_ref, f32[512,128]{1,0:T(8,128)S(1)} %copy-done, f32[2,512,1024]{2,1,0:T(8,128)} %field_ref.3), custom_call_target="tpu_custom_call" | custom-call | tf_op jit(solution)/shard_map/pallas_call | solution.py:271
  (6 shorter events, 0.1 us)
Async XLA Ops:
  0.6 54.9 %copy-start = (f32[512,128]{1,0:T(8,128)S(1)}, f32[512,128]{1,0:T(8,128)}, u32[]{:S(2)}) copy-start(f32[512,128]{1,0:T(8,128)} %start_ref.1) | copy-start | bytes 786436
  4.8 4.6 %collective-permute-start = (f32[640,128]{1,0:T(8,128)S(1)}, f32[640,128]{1,0:T(8,128)S(1)}, u32[]{:S(2)}, u32[]{:S(2)}) collective-permute-start(f32[640,128]{1,0:T(8,128)S(1)} %constant_dynamic-slice_fusion), channel_id=1, source_target_pairs={{0,1},{1,0},{2,3},{3,2},{4,5},{5,4},{6,7},{7,6},{8,9},{9,8},{10,11... | collective-permute-start | bytes 983048 | tf_op jit(solution)/shard_map/ppermute | solution.py:306
  50.4 5.2 %collective-permute-start.1 = (f32[640,128]{1,0:T(8,128)S(1)}, f32[640,128]{1,0:T(8,128)S(1)}, u32[]{:S(2)}, u32[]{:S(2)}) collective-permute-start(f32[640,128]{1,0:T(8,128)S(1)} %bitcast.6), channel_id=1, source_target_pairs={{0,1},{1,0},{2,3},{3,2},{4,5},{5,4},{6,7},{7,6},{8,9},{9,8},{10,11... | collective-permute-start | bytes 983048 | tf_op jit(solution)/shard_map/ppermute | solution.py:313

commit v5 on v4

--- a/solution.py
+++ b/solution.py
@@ -308,7 +308,8 @@
     piece = half // plane
     pieces = lax.all_to_all(own.reshape(plane, piece, BLOCK), ("y", "x"), 0, 0)
     own = jnp.sum(pieces, axis=0)
-    own = jnp.sum(spread(own, "z", lax.axis_size("z")), axis=0)
+    for flip in (1, 2, 7):
+        own = own + lax.ppermute(own, "z", [(i, i ^ flip) for i in range(lax.axis_size("z"))])
     own = spread(own, ("y", "x"), plane).reshape(half, BLOCK)
     return core, own, lax.ppermute(own, "core", swap)
 

time: 70.6 us -> 69.1 us (0.979)
  blocking collectives: 40.9 us -> 24.3 us
  starting transfers between devices: 7.22 us -> 18.7 us
  waiting for transfers between devices: 2.51 us -> 6.02 us
    all_to_all x2 -> x1, blocking collectives: 27.2 us -> 10.7 us  [spread(): lax.all_to_all(jnp.broadcast_to(block, (size,) + block.shape), axes, 0, 0)]
    ppermute x0 -> x3, starting transfers between devices: none -> 9.48 us  [all_sum(): lax.ppermute(own, 'z', [(i, i ^ flip) for i in range(lax.axis_size('z'))])]
    ppermute x0 -> x3, waiting for transfers between devices: none -> 3.51 us  [all_sum(): lax.ppermute(own, 'z', [(i, i ^ flip) for i in range(lax.axis_size('z'))])]
    ppermute x1, starting transfers between devices: 3.9 us -> 5.9 us  [all_sum(): return (core, own, lax.ppermute(own, 'core', swap))]
  transfers between devices with their start and end apart: 2 -> 5, of which waited for: 2 -> 5; matrix products, arithmetic and copies ran while one was open for 0% -> 0% of each run, Pallas kernels for 0% -> 0%
where the time goes in v5:
time: 69.1 us; the launch traced here: 68.9 us
  blocking collectives  24.3 us (35%)
  Pallas kernels  19 us (27%)
  starting transfers between devices  18.7 us (27%)
  waiting for transfers between devices  6.02 us (9%)
    pallas_call x1, Pallas kernels, sweeps(): pl.pallas_call(sweeps_kernel, in_specs=[pl.BlockSpec(memory_space=pltpu.S...  14.9 us
    all_to_all x1, blocking collectives, all_sum(): pieces = lax.all_to_all(own.reshape(plane, piece, BLOCK), ('y', 'x'), 0, 0)  13.6 us
    all_to_all x1, blocking collectives, spread(): lax.all_to_all(jnp.broadcast_to(block, (size,) + block.shape), axes, 0, 0)  10.7 us
    ppermute x3, starting transfers between devices, all_sum(): lax.ppermute(own, 'z', [(i, i ^ flip) for i in range(lax.axis_size('z'))])  9.48 us
    ppermute x1, starting transfers between devices, all_sum(): return (core, own, lax.ppermute(own, 'core', swap))  5.9 us
    pallas_call x1, Pallas kernels, partial_gram(): pl.pallas_call(gram_kernel, in_specs=[pl.BlockSpec(memory_space=pltpu.HBM...  4.11 us
    ppermute x3, waiting for transfers between devices, all_sum(): lax.ppermute(own, 'z', [(i, i ^ flip) for i in range(lax.axis_size('z'))])  3.51 us
    ppermute x1, starting transfers between devices, all_sum(): own = mine + lax.ppermute(theirs, 'core', swap)  3.32 us
  transfers between devices with their start and end apart: 5, of which 5 were waited for; matrix products, arithmetic and copies ran while one was open for 0% of the time, Pallas kernels for 0%

profile of v5, /device:TPU:1, one launch (start us, length us, event | category | flops | bytes accessed | tf_op | source)
XLA Modules:
  0.0 68.9 jit_solution(311609807597172021)
XLA Ops:
  0.6 0.0 copy-start
  0.6 4.1 %shard_map.41 = f32[10,128,128]{2,1,0:T(8,128)S(1)} custom-call(f32[2,512,1024]{2,1,0:T(8,128)} %field_ref.3), custom_call_target="tpu_custom_call" | custom-call | tf_op jit(solution)/shard_map/pallas_call | solution.py:59
  4.8 3.3 %collective-permute-start = (f32[640,128]{1,0:T(8,128)S(1)}, f32[640,128]{1,0:T(8,128)S(1)}, u32[]{:S(2)}, u32[]{:S(2)}) collective-permute-start(f32[640,128]{1,0:T(8,128)S(1)} %constant_dynamic-slice_fusion), channel_id=1, source_target_pairs={{0,1},{1,0},{2,3},{3,2},{4,5},{5,4},{6,7},{7,6},{8,9},{9,8},{10,11... | collective-permute-start | bytes 983048 | tf_op jit(solution)/shard_map/ppermute | solution.py:306
  8.1 1.3 %collective-permute-done = f32[640,128]{1,0:T(8,128)S(1)} collective-permute-done((f32[640,128]{1,0:T(8,128)S(1)}, f32[640,128]{1,0:T(8,128)S(1)}, u32[]{:S(2)}, u32[]{:S(2)}) %collective-permute-start) | collective-permute-done | bytes 327712 | tf_op jit(solution)/shard_map/ppermute | solution.py:306
  9.4 13.6 %all_to_all.10 = f32[16,40,128]{2,1,0:T(8,128)S(1)} all-to-all(f32[16,40,128]{2,1,0:T(8,128)S(1)} %bitcast.8), channel_id=1, replica_groups=mesh['z'=8,'y'=4,'x'=4,'core'=2] {'y','x'}, dimensions={0} | all-to-all | bytes 655360 | tf_op jit(solution)/shard_map/all_to_all | solution.py:309
  23.1 1.7 %collective-permute-start.1 = (f32[40,128]{1,0:T(8,128)S(1)}, f32[40,128]{1,0:T(8,128)S(1)}, u32[]{:S(2)}, u32[]{:S(2)}) collective-permute-start(f32[40,128]{1,0:T(8,128)S(1)} %reduce_sum.9), channel_id=1, source_target_pairs={{0,32},{32,0},{64,96},{96,64},{128,160},{160,128},{192,224},{224,1... | collective-permute-start | bytes 61448 | tf_op jit(solution)/shard_map/ppermute | solution.py:312
  24.8 1.2 %collective-permute-done.1 = f32[40,128]{1,0:T(8,128)S(1)} collective-permute-done((f32[40,128]{1,0:T(8,128)S(1)}, f32[40,128]{1,0:T(8,128)S(1)}, u32[]{:S(2)}, u32[]{:S(2)}) %collective-permute-start.1) | collective-permute-done | bytes 20512 | tf_op jit(solution)/shard_map/ppermute | solution.py:312
  26.0 3.0 %collective-permute-start.2 = (f32[40,128]{1,0:T(8,128)S(1)}, f32[40,128]{1,0:T(8,128)S(1)}, u32[]{:S(2)}, u32[]{:S(2)}) collective-permute-start(f32[40,128]{1,0:T(8,128)S(1)} %add.21), channel_id=1, source_target_pairs={{0,64},{32,96},{64,0},{96,32},{128,192},{160,224},{192,128},{224,1... | collective-permute-start | bytes 61448 | tf_op jit(solution)/shard_map/ppermute | solution.py:312
  29.0 1.2 %collective-permute-done.2 = f32[40,128]{1,0:T(8,128)S(1)} collective-permute-done((f32[40,128]{1,0:T(8,128)S(1)}, f32[40,128]{1,0:T(8,128)S(1)}, u32[]{:S(2)}, u32[]{:S(2)}) %collective-permute-start.2) | collective-permute-done | bytes 20512 | tf_op jit(solution)/shard_map/ppermute | solution.py:312
  30.1 4.8 %collective-permute-start.3 = (f32[40,128]{1,0:T(8,128)S(1)}, f32[40,128]{1,0:T(8,128)S(1)}, u32[]{:S(2)}, u32[]{:S(2)}) collective-permute-start(f32[40,128]{1,0:T(8,128)S(1)} %add.22), channel_id=1, source_target_pairs={{0,224},{32,192},{64,160},{96,128},{128,96},{160,64},{192,32},{224... | collective-permute-start | bytes 61448 | tf_op jit(solution)/shard_map/ppermute | solution.py:312
  34.9 1.2 %collective-permute-done.3 = f32[40,128]{1,0:T(8,128)S(1)} collective-permute-done((f32[40,128]{1,0:T(8,128)S(1)}, f32[40,128]{1,0:T(8,128)S(1)}, u32[]{:S(2)}, u32[]{:S(2)}) %collective-permute-start.3) | collective-permute-done | bytes 20512 | tf_op jit(solution)/shard_map/ppermute | solution.py:312
  36.1 10.7 %all_to_all.11 = f32[16,40,128]{2,1,0:T(8,128)S(1)} all-to-all(f32[16,40,128]{2,1,0:T(8,128)S(1)} %broadcast_in_dim.3), channel_id=1, replica_groups=mesh['z'=8,'y'=4,'x'=4,'core'=2] {'y','x'}, dimensions={0} | all-to-all | bytes 655360 | tf_op jit(solution)/shard_map/all_to_all | solution.py:297
  46.8 5.9 %collective-permute-start.4 = (f32[640,128]{1,0:T(8,128)S(1)}, f32[640,128]{1,0:T(8,128)S(1)}, u32[]{:S(2)}, u32[]{:S(2)}) collective-permute-start(f32[640,128]{1,0:T(8,128)S(1)} %bitcast.6), channel_id=1, source_target_pairs={{0,1},{1,0},{2,3},{3,2},{4,5},{5,4},{6,7},{7,6},{8,9},{9,8},{10,11... | collective-permute-start | bytes 983048 | tf_op jit(solution)/shard_map/ppermute | solution.py:314
  52.7 1.3 %collective-permute-done.4.other_ref = f32[640,128]{1,0:T(8,128)S(1)} collective-permute-done((f32[640,128]{1,0:T(8,128)S(1)}, f32[640,128]{1,0:T(8,128)S(1)}, u32[]{:S(2)}, u32[]{:S(2)}) %collective-permute-start.4) | collective-permute-done | bytes 327712 | tf_op jit(solution)/shard_map/ppermute | solution.py:314
  54.0 0.0 copy-done
  54.0 14.9 %shard_map.42 = (f32[2,128,1024]{2,1,0:T(8,128)}, f32[512,128]{1,0:T(8,128)}) custom-call(s32[1]{0:T(128)} %bitcast.core_ref, f32[640,128]{1,0:T(8,128)S(1)} %bitcast.7, f32[640,128]{1,0:T(8,128)S(1)} %collective-permute-done.4.other_ref, f32[512,128]{1,0:T(8,128)S(1)} %copy-done, f32[2,512,1024]{2,1,0:T(8,128)} %field_ref.3), custom_call_target="tpu_custom_call" | custom-call | tf_op jit(solution)/shard_map/pallas_call | solution.py:271
  (7 shorter events, 0.1 us)
Async XLA Ops:
  0.6 53.3 %copy-start = (f32[512,128]{1,0:T(8,128)S(1)}, f32[512,128]{1,0:T(8,128)}, u32[]{:S(2)}) copy-start(f32[512,128]{1,0:T(8,128)} %start_ref.1) | copy-start | bytes 786436
  4.8 4.6 %collective-permute-start = (f32[640,128]{1,0:T(8,128)S(1)}, f32[640,128]{1,0:T(8,128)S(1)}, u32[]{:S(2)}, u32[]{:S(2)}) collective-permute-start(f32[640,128]{1,0:T(8,128)S(1)} %constant_dynamic-slice_fusion), channel_id=1, source_target_pairs={{0,1},{1,0},{2,3},{3,2},{4,5},{5,4},{6,7},{7,6},{8,9},{9,8},{10,11... | collective-permute-start | bytes 983048 | tf_op jit(solution)/shard_map/ppermute | solution.py:306
  23.1 2.9 %collective-permute-start.1 = (f32[40,128]{1,0:T(8,128)S(1)}, f32[40,128]{1,0:T(8,128)S(1)}, u32[]{:S(2)}, u32[]{:S(2)}) collective-permute-start(f32[40,128]{1,0:T(8,128)S(1)} %reduce_sum.9), channel_id=1, source_target_pairs={{0,32},{32,0},{64,96},{96,64},{128,160},{160,128},{192,224},{224,1... | collective-permute-start | bytes 61448 | tf_op jit(solution)/shard_map/ppermute | solution.py:312
  26.0 4.2 %collective-permute-start.2 = (f32[40,128]{1,0:T(8,128)S(1)}, f32[40,128]{1,0:T(8,128)S(1)}, u32[]{:S(2)}, u32[]{:S(2)}) collective-permute-start(f32[40,128]{1,0:T(8,128)S(1)} %add.21), channel_id=1, source_target_pairs={{0,64},{32,96},{64,0},{96,32},{128,192},{160,224},{192,128},{224,1... | collective-permute-start | bytes 61448 | tf_op jit(solution)/shard_map/ppermute | solution.py:312
  30.1 6.0 %collective-permute-start.3 = (f32[40,128]{1,0:T(8,128)S(1)}, f32[40,128]{1,0:T(8,128)S(1)}, u32[]{:S(2)}, u32[]{:S(2)}) collective-permute-start(f32[40,128]{1,0:T(8,128)S(1)} %add.22), channel_id=1, source_target_pairs={{0,224},{32,192},{64,160},{96,128},{128,96},{160,64},{192,32},{224... | collective-permute-start | bytes 61448 | tf_op jit(solution)/shard_map/ppermute | solution.py:312
  46.8 7.2 %collective-permute-start.4 = (f32[640,128]{1,0:T(8,128)S(1)}, f32[640,128]{1,0:T(8,128)S(1)}, u32[]{:S(2)}, u32[]{:S(2)}) collective-permute-start(f32[640,128]{1,0:T(8,128)S(1)} %bitcast.6), channel_id=1, source_target_pairs={{0,1},{1,0},{2,3},{3,2},{4,5},{5,4},{6,7},{7,6},{8,9},{9,8},{10,11... | collective-permute-start | bytes 983048 | tf_op jit(solution)/shard_map/ppermute | solution.py:314

commit v6 on v5

--- a/solution.py
+++ b/solution.py
@@ -193,9 +193,8 @@
         block = jnp.where(own_first == (index * BLOCK < rows_half), own, other)
         for part, values in enumerate(split_three(block)):
             gram_ref[part, BLOCK * i : BLOCK * (i + 1), BLOCK * j : BLOCK * (j + 1)] = values
-        if i != j:
-            for part, values in enumerate(split_three(block.T)):
-                gram_ref[part, BLOCK * j : BLOCK * (j + 1), BLOCK * i : BLOCK * (i + 1)] = values
+            if i != j:
+                gram_ref[part, BLOCK * j : BLOCK * (j + 1), BLOCK * i : BLOCK * (i + 1)] = values.T
 
     def keep(ref, values, at=0):
         for part, piece in enumerate(split_three(values)):
@@ -210,15 +209,19 @@
         return by_high[:RANK] + (by_high[RANK : 2 * RANK] + by_middle[:RANK] + small)
 
     def products():
-        both = dot(image_ref[...], image_ref[: 2 * RANK, :], nt)
-        small = both[2 * RANK :, :RANK] + dot(image_ref[:RANK, :], image_ref[2 * RANK :, :], nt)
-        middle = both[:RANK, RANK:] + both[RANK : 2 * RANK, :RANK]
-        return both[:RANK, :RANK] + (middle + (both[RANK : 2 * RANK, RANK:] + small))
-
-    def times_inverse(inverse, ref):
+        total = 0.0
+        for at in (0, 256):
+            image = image_ref[:, at : at + 256]
+            both = dot(image, image[: 2 * RANK], nt)
+            small = both[2 * RANK :, :RANK] + dot(image[:RANK], image[2 * RANK :], nt)
+            middle = both[:RANK, RANK:] + both[RANK : 2 * RANK, :RANK]
+            total = total + (both[:RANK, :RANK] + (middle + (both[RANK : 2 * RANK, RANK:] + small)))
+        return total
+
+    def times_inverse(inverse, ref, span=slice(0, N1)):
         high, middle, low = split_three(inverse)
         left = jnp.concatenate([high, low, middle, middle, high, high], axis=1)
-        by_high, by_middle, by_low = (ref[RANK * part : RANK * (part + 1), :] for part in range(3))
+        by_high, by_middle, by_low = (ref[RANK * part : RANK * (part + 1), span] for part in range(3))
         right = jnp.concatenate([by_low, by_high, by_middle, by_high, by_middle, by_high], axis=0)
         return dot(left, right, nn)
 
@@ -231,7 +234,8 @@
                 keep(ahead_ref, times_gram(128 * r, 256), 128 * r)
 
         inverse = inverse_factor(products(), beside)
-        keep(image_ref, times_inverse(inverse, ahead_ref))
+        for at in (0, 256):
+            keep(image_ref, times_inverse(inverse, ahead_ref, slice(at, at + 256)), at)
         return carry
 
     lax.fori_loop(0, ITERS - 1, sweep, 0)

time: 69.1 us -> 68.4 us (0.990)
  no operation moved by 1% of the time
where the time goes in v6:
time: 68.4 us; the launch traced here: 68.2 us
  blocking collectives  24.3 us (36%)
  starting transfers between devices  18.7 us (27%)
  Pallas kernels  18.4 us (27%)
  waiting for transfers between devices  6.02 us (9%)
    pallas_call x1, Pallas kernels, sweeps(): pl.pallas_call(sweeps_kernel, in_specs=[pl.BlockSpec(memory_space=pltpu.S...  14.3 us
    all_to_all x1, blocking collectives, all_sum(): pieces = lax.all_to_all(own.reshape(plane, piece, BLOCK), ('y', 'x'), 0, 0)  13.6 us
    all_to_all x1, blocking collectives, spread(): lax.all_to_all(jnp.broadcast_to(block, (size,) + block.shape), axes, 0, 0)  10.7 us
    ppermute x3, starting transfers between devices, all_sum(): lax.ppermute(own, 'z', [(i, i ^ flip) for i in range(lax.axis_size('z'))])  9.48 us
    ppermute x1, starting transfers between devices, all_sum(): return (core, own, lax.ppermute(own, 'core', swap))  5.9 us
    pallas_call x1, Pallas kernels, partial_gram(): pl.pallas_call(gram_kernel, in_specs=[pl.BlockSpec(memory_space=pltpu.HBM...  4.11 us
    ppermute x3, waiting for transfers between devices, all_sum(): lax.ppermute(own, 'z', [(i, i ^ flip) for i in range(lax.axis_size('z'))])  3.51 us
    ppermute x1, starting transfers between devices, all_sum(): own = mine + lax.ppermute(theirs, 'core', swap)  3.32 us
  transfers between devices with their start and end apart: 5, of which 5 were waited for; matrix products, arithmetic and copies ran while one was open for 0% of the time, Pallas kernels for 0%

profile of v6, /device:TPU:1, one launch (start us, length us, event | category | flops | bytes accessed | tf_op | source)
XLA Modules:
  0.0 68.2 jit_solution(13912597830600003445)
XLA Ops:
  0.6 0.0 copy-start
  0.6 4.1 %shard_map.41 = f32[10,128,128]{2,1,0:T(8,128)S(1)} custom-call(f32[2,512,1024]{2,1,0:T(8,128)} %field_ref.3), custom_call_target="tpu_custom_call" | custom-call | tf_op jit(solution)/shard_map/pallas_call | solution.py:59
  4.8 3.3 %collective-permute-start = (f32[640,128]{1,0:T(8,128)S(1)}, f32[640,128]{1,0:T(8,128)S(1)}, u32[]{:S(2)}, u32[]{:S(2)}) collective-permute-start(f32[640,128]{1,0:T(8,128)S(1)} %constant_dynamic-slice_fusion), channel_id=1, source_target_pairs={{0,1},{1,0},{2,3},{3,2},{4,5},{5,4},{6,7},{7,6},{8,9},{9,8},{10,11... | collective-permute-start | bytes 983048 | tf_op jit(solution)/shard_map/ppermute | solution.py:310
  8.1 1.3 %collective-permute-done = f32[640,128]{1,0:T(8,128)S(1)} collective-permute-done((f32[640,128]{1,0:T(8,128)S(1)}, f32[640,128]{1,0:T(8,128)S(1)}, u32[]{:S(2)}, u32[]{:S(2)}) %collective-permute-start) | collective-permute-done | bytes 327712 | tf_op jit(solution)/shard_map/ppermute | solution.py:310
  9.4 13.6 %all_to_all.10 = f32[16,40,128]{2,1,0:T(8,128)S(1)} all-to-all(f32[16,40,128]{2,1,0:T(8,128)S(1)} %bitcast.8), channel_id=1, replica_groups=mesh['z'=8,'y'=4,'x'=4,'core'=2] {'y','x'}, dimensions={0} | all-to-all | bytes 655360 | tf_op jit(solution)/shard_map/all_to_all | solution.py:313
  23.1 1.7 %collective-permute-start.1 = (f32[40,128]{1,0:T(8,128)S(1)}, f32[40,128]{1,0:T(8,128)S(1)}, u32[]{:S(2)}, u32[]{:S(2)}) collective-permute-start(f32[40,128]{1,0:T(8,128)S(1)} %reduce_sum.9), channel_id=1, source_target_pairs={{0,32},{32,0},{64,96},{96,64},{128,160},{160,128},{192,224},{224,1... | collective-permute-start | bytes 61448 | tf_op jit(solution)/shard_map/ppermute | solution.py:316
  24.8 1.2 %collective-permute-done.1 = f32[40,128]{1,0:T(8,128)S(1)} collective-permute-done((f32[40,128]{1,0:T(8,128)S(1)}, f32[40,128]{1,0:T(8,128)S(1)}, u32[]{:S(2)}, u32[]{:S(2)}) %collective-permute-start.1) | collective-permute-done | bytes 20512 | tf_op jit(solution)/shard_map/ppermute | solution.py:316
  26.0 3.0 %collective-permute-start.2 = (f32[40,128]{1,0:T(8,128)S(1)}, f32[40,128]{1,0:T(8,128)S(1)}, u32[]{:S(2)}, u32[]{:S(2)}) collective-permute-start(f32[40,128]{1,0:T(8,128)S(1)} %add.21), channel_id=1, source_target_pairs={{0,64},{32,96},{64,0},{96,32},{128,192},{160,224},{192,128},{224,1... | collective-permute-start | bytes 61448 | tf_op jit(solution)/shard_map/ppermute | solution.py:316
  29.0 1.2 %collective-permute-done.2 = f32[40,128]{1,0:T(8,128)S(1)} collective-permute-done((f32[40,128]{1,0:T(8,128)S(1)}, f32[40,128]{1,0:T(8,128)S(1)}, u32[]{:S(2)}, u32[]{:S(2)}) %collective-permute-start.2) | collective-permute-done | bytes 20512 | tf_op jit(solution)/shard_map/ppermute | solution.py:316
  30.1 4.8 %collective-permute-start.3 = (f32[40,128]{1,0:T(8,128)S(1)}, f32[40,128]{1,0:T(8,128)S(1)}, u32[]{:S(2)}, u32[]{:S(2)}) collective-permute-start(f32[40,128]{1,0:T(8,128)S(1)} %add.22), channel_id=1, source_target_pairs={{0,224},{32,192},{64,160},{96,128},{128,96},{160,64},{192,32},{224... | collective-permute-start | bytes 61448 | tf_op jit(solution)/shard_map/ppermute | solution.py:316
  34.9 1.2 %collective-permute-done.3 = f32[40,128]{1,0:T(8,128)S(1)} collective-permute-done((f32[40,128]{1,0:T(8,128)S(1)}, f32[40,128]{1,0:T(8,128)S(1)}, u32[]{:S(2)}, u32[]{:S(2)}) %collective-permute-start.3) | collective-permute-done | bytes 20512 | tf_op jit(solution)/shard_map/ppermute | solution.py:316
  36.1 10.7 %all_to_all.11 = f32[16,40,128]{2,1,0:T(8,128)S(1)} all-to-all(f32[16,40,128]{2,1,0:T(8,128)S(1)} %broadcast_in_dim.3), channel_id=1, replica_groups=mesh['z'=8,'y'=4,'x'=4,'core'=2] {'y','x'}, dimensions={0} | all-to-all | bytes 655360 | tf_op jit(solution)/shard_map/all_to_all | solution.py:301
  46.8 5.9 %collective-permute-start.4 = (f32[640,128]{1,0:T(8,128)S(1)}, f32[640,128]{1,0:T(8,128)S(1)}, u32[]{:S(2)}, u32[]{:S(2)}) collective-permute-start(f32[640,128]{1,0:T(8,128)S(1)} %bitcast.6), channel_id=1, source_target_pairs={{0,1},{1,0},{2,3},{3,2},{4,5},{5,4},{6,7},{7,6},{8,9},{9,8},{10,11... | collective-permute-start | bytes 983048 | tf_op jit(solution)/shard_map/ppermute | solution.py:318
  52.7 1.3 %collective-permute-done.4.other_ref = f32[640,128]{1,0:T(8,128)S(1)} collective-permute-done((f32[640,128]{1,0:T(8,128)S(1)}, f32[640,128]{1,0:T(8,128)S(1)}, u32[]{:S(2)}, u32[]{:S(2)}) %collective-permute-start.4) | collective-permute-done | bytes 327712 | tf_op jit(solution)/shard_map/ppermute | solution.py:318
  54.0 0.0 copy-done
  54.0 14.3 %shard_map.42 = (f32[2,128,1024]{2,1,0:T(8,128)}, f32[512,128]{1,0:T(8,128)}) custom-call(s32[1]{0:T(128)} %bitcast.core_ref, f32[640,128]{1,0:T(8,128)S(1)} %bitcast.7, f32[640,128]{1,0:T(8,128)S(1)} %collective-permute-done.4.other_ref, f32[512,128]{1,0:T(8,128)S(1)} %copy-done, f32[2,512,1024]{2,1,0:T(8,128)} %field_ref.3), custom_call_target="tpu_custom_call" | custom-call | tf_op jit(solution)/shard_map/pallas_call | solution.py:275
  (7 shorter events, 0.1 us)
Async XLA Ops:
  0.6 53.3 %copy-start = (f32[512,128]{1,0:T(8,128)S(1)}, f32[512,128]{1,0:T(8,128)}, u32[]{:S(2)}) copy-start(f32[512,128]{1,0:T(8,128)} %start_ref.1) | copy-start | bytes 786436
  4.8 4.6 %collective-permute-start = (f32[640,128]{1,0:T(8,128)S(1)}, f32[640,128]{1,0:T(8,128)S(1)}, u32[]{:S(2)}, u32[]{:S(2)}) collective-permute-start(f32[640,128]{1,0:T(8,128)S(1)} %constant_dynamic-slice_fusion), channel_id=1, source_target_pairs={{0,1},{1,0},{2,3},{3,2},{4,5},{5,4},{6,7},{7,6},{8,9},{9,8},{10,11... | collective-permute-start | bytes 983048 | tf_op jit(solution)/shard_map/ppermute | solution.py:310
  23.1 2.9 %collective-permute-start.1 = (f32[40,128]{1,0:T(8,128)S(1)}, f32[40,128]{1,0:T(8,128)S(1)}, u32[]{:S(2)}, u32[]{:S(2)}) collective-permute-start(f32[40,128]{1,0:T(8,128)S(1)} %reduce_sum.9), channel_id=1, source_target_pairs={{0,32},{32,0},{64,96},{96,64},{128,160},{160,128},{192,224},{224,1... | collective-permute-start | bytes 61448 | tf_op jit(solution)/shard_map/ppermute | solution.py:316
  26.0 4.2 %collective-permute-start.2 = (f32[40,128]{1,0:T(8,128)S(1)}, f32[40,128]{1,0:T(8,128)S(1)}, u32[]{:S(2)}, u32[]{:S(2)}) collective-permute-start(f32[40,128]{1,0:T(8,128)S(1)} %add.21), channel_id=1, source_target_pairs={{0,64},{32,96},{64,0},{96,32},{128,192},{160,224},{192,128},{224,1... | collective-permute-start | bytes 61448 | tf_op jit(solution)/shard_map/ppermute | solution.py:316
  30.1 6.0 %collective-permute-start.3 = (f32[40,128]{1,0:T(8,128)S(1)}, f32[40,128]{1,0:T(8,128)S(1)}, u32[]{:S(2)}, u32[]{:S(2)}) collective-permute-start(f32[40,128]{1,0:T(8,128)S(1)} %add.22), channel_id=1, source_target_pairs={{0,224},{32,192},{64,160},{96,128},{128,96},{160,64},{192,32},{224... | collective-permute-start | bytes 61448 | tf_op jit(solution)/shard_map/ppermute | solution.py:316
  46.8 7.2 %collective-permute-start.4 = (f32[640,128]{1,0:T(8,128)S(1)}, f32[640,128]{1,0:T(8,128)S(1)}, u32[]{:S(2)}, u32[]{:S(2)}) collective-permute-start(f32[640,128]{1,0:T(8,128)S(1)} %bitcast.6), channel_id=1, source_target_pairs={{0,1},{1,0},{2,3},{3,2},{4,5},{5,4},{6,7},{7,6},{8,9},{9,8},{10,11... | collective-permute-start | bytes 983048 | tf_op jit(solution)/shard_map/ppermute | solution.py:318
